TPU v7x, 128 devices: a whole 4x4x4 slice. The times are simulated.
128 devices in a mesh: section: 2 (over core), dp: 16 (over y, x), tensor: 4 (over z).
Axes of the slice: x: 4, y: 4, z: 4, core: 2. Of those that a mesh axis runs over, the one named last changes fastest.
Arguments:
- section_ends: bfloat16 [2, 2, 8192, 1536], P('section', None, ('dp', 'tensor')), may hold values from -6 to 6
- norm_gain: bfloat16 [2, 1536], P('section', ('dp', 'tensor')), may hold values from 0.5 to 1.5
- proj_inner: bfloat16 [2, 1536, 2, 3072], P('section', 'dp', None, 'tensor'), may hold values from -0.15625 to 0.15625
- proj_step: bfloat16 [2, 1536, 48], P('section', 'dp', 'tensor'), may hold values from -0.15625 to 0.15625
- proj_state: bfloat16 [2, 1536, 256], P('section', ('dp', 'tensor')), may hold values from -0.15625 to 0.15625
- conv_inner: bfloat16 [2, 5, 3072], P('section', None, ('dp', 'tensor')), may hold values from -0.5 to 0.5
- conv_state: bfloat16 [2, 5, 256], P('section', None, ('dp', 'tensor')), may hold values from -0.5 to 0.5
- gate_gain: bfloat16 [2, 3072], P('section', ('dp', 'tensor')), may hold values from 0.5 to 1.5
- head_params: bfloat16 [2, 3, 48], P('section', None, 'tensor'), may hold values from -5 to 1.5, as said below
- proj_output: bfloat16 [2, 3072, 1536], P('section', 'tensor', 'dp'), may hold values from -0.109375 to 0.109375
Outputs:
- section_results: float32 [2, 2, 8192, 1536], P('section', None, ('dp', 'tensor'))
- grad_norm_gain: float32 [2, 1536], P('section', ('dp', 'tensor'))
- grad_proj_inner: float32 [2, 1536, 2, 3072], P('section', 'dp', None, 'tensor')
- grad_proj_step: float32 [2, 1536, 48], P('section', 'dp', 'tensor')
- grad_proj_state: float32 [2, 1536, 256], P('section', ('dp', 'tensor'))
- grad_conv_inner: float32 [2, 5, 3072], P('section', None, ('dp', 'tensor'))
- grad_conv_state: float32 [2, 5, 256], P('section', None, ('dp', 'tensor'))
- grad_gate_gain: float32 [2, 3072], P('section', ('dp', 'tensor'))
- grad_head_params: float32 [2, 3, 48], P('section', None, 'tensor')
- grad_proj_output: float32 [2, 3072, 1536], P('section', 'tensor', 'dp')
Inputs may be any that keep to these rules, and one draw needn't show every extreme that they name: `head_params`: row 0 lies in -5 to -1, row 1 in -1 to 1.5, row 2 in 0.5 to 1.5.
All inputs are finite; a program needn't handle non-finite values.
Results may differ from a plain program's by a relative error of at most 0.018.
Values may be sent and summed in bfloat16 or wider, within the bound.
No kernel may reach another device: no remote copies, remote signals or barrier semaphores. Data moves between devices by JAX's collectives and lax.ppermute only.
A program may use at most 192 MiB of HBM per device.

v0:
```python
import jax
import jax.numpy as jnp
from jax import lax
from jax.experimental import pallas as pl
from jax.experimental.pallas import tpu as pltpu
from jax.sharding import Mesh
from jax.sharding import PartitionSpec as P

D = 1536
SEQ = 512
BLOCK = 128
BLOCKS = SEQ // BLOCK
STATES = 128
CHANNELS = 768
HEADS = 12
HEAD_DIM = 64
PAIRS = HEADS // 2
DI = 3072
PAD = 8
EPS = 1e-05
NEG = -1e30
DP = ("dp_0", "dp_1")
DP_TENSOR = ("dp_0", "dp_1", "tensor")
SENT = D + 128
BF = jnp.bfloat16
F32 = jnp.float32
HIGH = lax.Precision.HIGHEST
VMEM = pl.BlockSpec(memory_space=pltpu.VMEM)
SMEM = pl.BlockSpec(memory_space=pltpu.SMEM)
HBM = pl.BlockSpec(memory_space=pltpu.HBM)
ANY = pl.BlockSpec(memory_space=pl.ANY)
SIDE = D // 2
WIDE = 2 * CHANNELS + CHANNELS + 384
IN = slice(0, 2 * CHANNELS)
OUT = slice(2 * CHANNELS, 3 * CHANNELS)
SS = slice(3 * CHANNELS, WIDE)
STATE = slice(3 * CHANNELS, 3 * CHANNELS + 256)
MISC = slice(3 * CHANNELS + 256, WIDE)
MAIN = 3 * CHANNELS
SPLIT = 2 * CHANNELS
PART = 256
LEFT, RIGHT = slice(0, SPLIT), slice(SPLIT, WIDE)
VMEM_LIMIT = 54


def shape(*dims, dtype=F32):
    return jax.ShapeDtypeStruct(dims, dtype)


def limit(megabytes):
    return pltpu.CompilerParams(vmem_limit_bytes=megabytes * 1024 * 1024)


def cost(flops, read):
    return pl.CostEstimate(flops=flops, bytes_accessed=read, transcendentals=0)


def dot_nn(left, right):
    return lax.dot_general(left, right, (((1,), (0,)), ((), ())), preferred_element_type=F32)


def dot_nt(left, right):
    return lax.dot_general(left, right, (((1,), (1,)), ((), ())), preferred_element_type=F32)


def dot_tn(left, right):
    return lax.dot_general(left, right, (((0,), (0,)), ((), ())), preferred_element_type=F32)


def dot_high(left, right):
    return lax.dot_general(
        left, right, (((1,), (0,)), ((), ())), precision=HIGH, preferred_element_type=F32
    )


def sigmoid(v):
    return 1.0 / (1.0 + jnp.exp(-v))


def softplus(v):
    return jnp.maximum(v, 0.0) + jnp.log1p(jnp.exp(-jnp.abs(v)))


def rows_at(index):
    return pl.ds(pl.multiple_of(index * BLOCK, BLOCK), BLOCK)


def lanes_at(index):
    return pl.ds(pl.multiple_of(index * 128, 128), 128)


def iota(shape, dim):
    return lax.broadcasted_iota(jnp.int32, shape, dim)


def two_parts(v):
    upper = v.astype(BF)
    lower = (v - upper.astype(F32)).astype(BF)
    return upper, lower


def lane_tiles(width):
    return [slice(at, at + 128) for at in range(0, width, 128)]


def conv_rows(padded, taps, out):
    for cols in lane_tiles(out.shape[1]):
        for start in range(0, SEQ, BLOCK):
            total = taps[4:5, cols] + taps[0:1, cols] * padded[start + 5 : start + 5 + BLOCK, cols]
            for k in range(1, 4):
                at = start + 5 + k
                total = total + taps[k : k + 1, cols] * padded[at : at + BLOCK, cols]
            out[start : start + BLOCK, cols] = total


def conv_back(padded_grad, padded, taps, grad_taps, store):
    for cols in lane_tiles(padded.shape[1]):
        sums = [jnp.zeros((1, 128), F32)] * 5
        for start in range(0, SEQ, BLOCK):
            own = padded_grad[start : start + BLOCK, cols]
            total = taps[3:4, cols] * own
            sums[4] = sums[4] + jnp.sum(own, axis=0, keepdims=True)
            for k in range(4):
                at = start + 5 + k
                sums[k] = sums[k] + jnp.sum(own * padded[at : at + BLOCK, cols], axis=0, keepdims=True)
                if k < 3:
                    at = start + 3 - k
                    total = total + taps[k : k + 1, cols] * padded_grad[at : at + BLOCK, cols]
            store(start, cols, total.astype(BF))
        for k in range(5):
            grad_taps[k : k + 1, cols] = sums[k]


def step_terms(raw, heads):
    valid = iota((BLOCK, 128), 1) < HEADS
    raised = jnp.where(valid, raw + heads[0:1, :], -30.0)
    step = softplus(raised)
    log_decay = -step * jnp.exp(heads[1:2, :])
    lower = (iota((BLOCK, BLOCK), 0) >= iota((BLOCK, BLOCK), 1)).astype(F32)
    summed = dot_high(lower, log_decay)
    return raised, step, log_decay, summed, jnp.transpose(summed)


def spread(values, head):
    first = iota((BLOCK, 128), 1) < HEAD_DIM
    return jnp.where(first, values[:, head : head + 1], values[:, head + 1 : head + 2])


def side_by_side(v):
    first = iota(v.shape, 1) < HEAD_DIM
    zero = jnp.zeros_like(v)
    return jnp.concatenate([jnp.where(first, v, zero), jnp.where(first, zero, v)], axis=0)


def over_96(v):
    return lax.shift_right_logical(v * 683, 16)


def select_lines(half):
    row, channel = iota((384, CHANNELS), 0), iota((384, CHANNELS), 1)
    return (channel == over_96(row) * 96 + row + 96 * half).astype(BF)


def select_state(rows, first):
    row, channel = iota((rows, 256), 0) + first, iota((rows, 256), 1)
    group = over_96(row)
    inside = row - 96 * group
    return ((inside < 16) & (channel == 16 * group + inside)).astype(BF)


def small_params(place, misc, heads_ref, taps, taps_state, gain):
    lines = misc[pl.ds(pl.multiple_of(place * 384, 128), 384), :]
    first = dot_tn(lines, select_lines(0))
    second = dot_tn(lines, select_lines(1))
    picks = (iota((128, CHANNELS), 0) == iota((128, CHANNELS), 1) // HEAD_DIM).astype(BF)
    skip = dot_nn(heads_ref[...].astype(BF), picks)
    taps[0:6, :] = first[12:18, :] + second[18:24, :]
    taps[6:7, :] = skip[2:3, :]
    taps[7:8, :] = jnp.zeros((1, CHANNELS), F32)
    taps_state[...] = jnp.zeros((8, 256), F32)
    taps_state[0:5, :] = dot_tn(misc[...], select_state(D, 0))[25:30, :]
    gain[...] = jnp.transpose(misc[...].astype(F32))[24:25, :]


SMALL = (shape(8, CHANNELS), shape(8, 256), shape(1, D))


class Copies:
    def __init__(self, sems):
        self.sems = sems
        self.count = 0
        self.pending = []

    def start(self, source, target):
        copy = pltpu.make_async_copy(source, target, self.sems.at[self.count])
        self.count += 1
        copy.start()
        return copy

    def store(self, source, target):
        self.pending.append(self.start(source, target))

    def finish(self):
        for copy in self.pending:
            copy.wait()


def place_blocks(copies, where_ref, parts, whole, cols):
    row, col = where_ref[2], where_ref[3]
    started = []
    for k, pieces in enumerate(parts):
        core = where_ref[1] if k == 0 else 1 - where_ref[1]
        if len(pieces) == 1:
            for at in range(16):
                spot = pl.ds(pl.multiple_of(at * 96 + 48 * core, 16), 48)
                source = pieces[0].at[at * 48 : (at + 1) * 48, cols]
                started.append(copies.start(source, whole.at[spot, cols]))
            continue
        own, ahead, far_left, far_right, behind = pieces
        far, shifted = far_left, cols
        if cols.start >= SPLIT:
            far, shifted = far_right, slice(cols.start - SPLIT, cols.stop - SPLIT)
        for o in range(4):
            part = slice(o * 48, (o + 1) * 48)
            for q in range(4):
                along = lax.rem(row + o, 4) * 4 + lax.rem(col + q, 4)
                across = lax.rem(row + q, 4) * 4 + lax.rem(col + o, 4)
                at = along + core * (across - along)
                spot = pl.ds(pl.multiple_of(at * 96 + 48 * core, 16), 48)
                if q == 2:
                    source = far.at[part, shifted]
                else:
                    source = {0: own, 1: ahead, 3: behind}[q].at[part, cols]
                started.append(copies.start(source, whole.at[spot, cols]))
    return started


def forward_kernel(last, *refs):
    refs = list(refs)

    def take(n):
        taken, refs[:n] = refs[:n], []
        return taken

    where_ref, ends = take(2)
    if last:
        chunks, own_in, other_in = take(4), take(1), take(1)
        taps_ref, taps_state_ref, heads_ref, gain_ref = take(4)
    else:
        own_in, other_in, (heads_ref,) = take(5), take(5), take(1)
    normed_out, zx_out, ss_out, y_out, starts_out, gg_out = take(6)
    if last:
        dscaled_out, stats, mixed_out = take(3)
    else:
        outs = take(4)
        taps_ref, taps_state_ref, gain_ref = take(3)
    normed, zx, ss, y_all, starts, gated_gain, whole = take(7)
    x_pad, state_pad, x_conv, state_conv, hidden, sems, held_rows = take(7)
    if last:
        dscaled, mixed = take(2)
    copies = Copies(sems)
    place, core = where_ref[0], where_ref[1]
    weights = (own_in, other_in)
    if not last:
        load_rows = [
            copies.start(ends.at[k, 0], held_rows.at[rows_at(k), :]) for k in range(BLOCKS)
        ]
        load_rest = place_blocks(copies, where_ref, weights, whole, RIGHT)
    load_in = place_blocks(copies, where_ref, weights, whole, LEFT)
    if last:
        load_rest = place_blocks(copies, where_ref, weights, whole, RIGHT)
    else:
        for load in load_rest + load_rows:
            load.wait()
        small_params(place, whole.at[:, MISC], heads_ref, taps_ref, taps_state_ref, gain_ref)
    for k, offset in enumerate((0, 3, 1, 2)):
        rows = rows_at(lax.rem(place + offset, 4))
        v = (chunks[k][...] if last else held_rows[rows, :]).astype(F32)
        q = lax.rsqrt(jnp.mean(v * v, axis=1, keepdims=True) + EPS)
        normed[rows, :] = (v * q * gain_ref[...]).astype(BF)
    copies.store(normed, normed_out)
    if last:
        load_rows = [
            copies.start(ends.at[k, 1], held_rows.at[rows_at(k), :]) for k in range(BLOCKS)
        ]
    for load in load_in:
        load.wait()
    zx[...] = dot_nn(normed[...], whole[:, IN])
    copies.store(zx, zx_out)
    if last:
        for load in load_rest + load_rows:
            load.wait()
    ss[...] = dot_nn(normed[...], whole[:, SS])
    copies.store(ss, ss_out)
    if last:
        dscaled[...] = dot_nn(held_rows[...], whole[:, OUT])
        copies.store(dscaled, dscaled_out)
    x_pad[:PAD, :] = jnp.zeros((PAD, CHANNELS), F32)
    x_pad[PAD:, :] = zx[:, CHANNELS:]
    state_pad[:PAD, :] = jnp.zeros((PAD, 2 * STATES), F32)
    state_pad[PAD:, :] = ss[:, : 2 * STATES]
    hidden[...] = jnp.zeros_like(hidden)
    conv_rows(x_pad, taps_ref, x_conv)
    conv_rows(state_pad, taps_state_ref, state_conv)

    def block(b, carry):
        rows = rows_at(b)
        state_u = state_conv[rows, :]
        state = state_u * sigmoid(state_u)
        keys, reads = state[:, :STATES].astype(BF), state[:, STATES:].astype(BF)
        keys_t = jnp.transpose(state[:, :STATES]).astype(BF)
        _, step, _, summed, summed_t = step_terms(ss[rows, 2 * STATES :], heads_ref)
        meets = dot_nt(reads, keys)
        causal = iota((BLOCK, BLOCK), 0) >= iota((BLOCK, BLOCK), 1)
        squares = jnp.zeros((BLOCK, 128), F32)
        crosses = jnp.zeros((BLOCK, 128), F32)
        for p in range(PAIRS):
            cols = slice(p * 128, (p + 1) * 128)
            u = x_conv[rows, cols]
            x = u * sigmoid(u)
            weighted = x * spread(step, 2 * p)
            summed_wide = spread(summed, 2 * p)
            grown = jnp.exp(summed_wide)
            to_end = jnp.exp(summed_wide[BLOCK - 1 : BLOCK, :] - summed_wide)
            mixes = []
            for h in (2 * p, 2 * p + 1):
                gaps = summed[:, h : h + 1] - summed_t[h : h + 1, :]
                mixes.append((jnp.exp(jnp.where(causal, gaps, NEG)) * meets).astype(BF))
            within = dot_nn(
                jnp.concatenate(mixes, axis=1), side_by_side(weighted).astype(BF)
            )
            held = hidden[:, cols]
            held_low = held.astype(BF)
            starts[b, :, cols] = held_low
            y = within + grown * dot_nn(reads, held_low) + x * taps_ref[6:7, cols]
            hidden[:, cols] = grown[BLOCK - 1 : BLOCK, :] * held + dot_nn(
                keys_t, (to_end * weighted).astype(BF)
            )
            y_all[rows, cols] = y
            z = zx[rows, cols]
            gated = y * z * sigmoid(z)
            squares = squares + gated * gated
            gained = gated * taps_ref[5:6, cols]
            gated_gain[rows, cols] = gained.astype(BF)
            if last:
                crosses = crosses + gained * dscaled[rows, cols]
        square = jnp.sum(squares, axis=1, keepdims=True)
        upper, lower = two_parts(square)
        lane = iota((BLOCK, 128), 1)
        zero = jnp.zeros((BLOCK, 128), F32)
        tail = jnp.where(
            lane == 0, upper.astype(F32), jnp.where(lane == 1, lower.astype(F32), zero)
        ).astype(BF)
        for o, out in enumerate(() if last else outs):

            @pl.when(b == lax.rem(place + o, 4))
            def _(out=out):
                out[:, D:] = tail

        if last:
            cross = jnp.sum(crosses, axis=1, keepdims=True)
            both = jnp.where(lane == 0, square, jnp.where(lane == 1, cross, zero))
            stats[:, rows] = jnp.transpose(both)[:8, :]
        return carry

    lax.fori_loop(0, BLOCKS, block, 0)
    copies.store(y_all, y_out)
    copies.store(starts, starts_out)
    copies.store(gated_gain, gg_out)
    for at in range(0, D, PART):
        cols = slice(at, at + PART)
        part = dot_nt(gated_gain[...], whole[cols, OUT]).astype(BF)
        target = mixed if last else held_rows
        target[:, cols] = part
    if last:
        copies.store(mixed, mixed_out)
    else:
        for o in range(4):
            outs[o][:, :D] = held_rows[rows_at(lax.rem(place + o, 4)), :]
    copies.finish()


def in_hbm(shapes):
    return [pltpu.HBM(k.shape, k.dtype) for k in shapes]


def forward_call(where, ends, chunks, weights):
    last = len(chunks) > 0
    kept = [
        shape(SEQ, D, dtype=BF),
        shape(SEQ, 2 * CHANNELS),
        shape(SEQ, 384),
        shape(SEQ, CHANNELS),
        shape(BLOCKS, STATES, CHANNELS, dtype=BF),
        shape(SEQ, CHANNELS, dtype=BF),
    ]
    out_shape, out_specs = in_hbm(kept), [HBM] * 6
    scratch = [pltpu.VMEM(k.shape, k.dtype) for k in kept] + [pltpu.VMEM((D, WIDE), BF)]
    scratch += [
        pltpu.VMEM((PAD + SEQ, CHANNELS), F32),
        pltpu.VMEM((PAD + SEQ, 2 * STATES), F32),
        pltpu.VMEM((SEQ, CHANNELS), F32),
        pltpu.VMEM((SEQ, 2 * STATES), F32),
        pltpu.VMEM((STATES, CHANNELS), F32),
        pltpu.SemaphoreType.DMA((96,)),
        pltpu.VMEM((SEQ, D), BF),
    ]
    if last:
        args = (where, ends, *chunks, *weights)
        in_specs = [SMEM, ANY] + [VMEM] * 4 + [ANY] * 2 + [VMEM] * 4
        more = [shape(SEQ, CHANNELS), shape(SEQ, D, dtype=BF)]
        out_shape += in_hbm(more[:1]) + [shape(8, SEQ)] + in_hbm(more[1:])
        out_specs += [HBM, VMEM, HBM]
        scratch += [pltpu.VMEM(k.shape, k.dtype) for k in more]
    else:
        args = (where, ends, *weights)
        in_specs = [SMEM, ANY] + [ANY] * 10 + [VMEM]
        out_shape += [shape(BLOCK, SENT, dtype=BF)] * 4 + list(SMALL)
        out_specs += [VMEM] * 7

    def kernel(*refs):
        forward_kernel(last, *refs)

    return pl.pallas_call(
        kernel,
        out_shape=out_shape,
        in_specs=in_specs,
        out_specs=out_specs,
        scratch_shapes=scratch,
        compiler_params=limit(VMEM_LIMIT),
        cost_estimate=cost(20 * 10**9, 24 * 10**6),
        name="layer_forward",
    )(*args)


def scaled_rows(rows_grad, factor):
    return (rows_grad.astype(F32) * factor).astype(BF)


def misc_parts(grad_small):
    taps_low = grad_small[0:8, 0:CHANNELS].astype(BF)
    lane, rank = iota((128, 8), 0), iota((128, 8), 1)
    lines = jnp.zeros((384, 128), F32)
    for half in range(2):
        put = ((lane == 12 + 6 * half + rank) & (rank < 6)).astype(BF)
        lines = lines + dot_nt(select_lines(half), dot_nn(put, taps_low).astype(BF))
    put = ((lane == 25 + rank) & (rank < 5)).astype(BF)
    state_low = grad_small[0:8, CHANNELS : CHANNELS + 256].astype(BF)
    state_lines = dot_nn(put, state_low).astype(BF)
    put = ((lane == 30 + rank) & (rank < 3)).astype(BF)
    heads_low = grad_small[0:8, CHANNELS + 256 : CHANNELS + 384].astype(BF)
    head_lines = dot_nn(put, heads_low).astype(BF)
    row, head = iota((384, 128), 0), iota((384, 128), 1)
    head_rows = ((row - 96 * over_96(row) == head) & (head < HEADS)).astype(BF)
    return lines, state_lines, dot_nt(head_rows, head_lines)


def misc_tile(i, place, parts, grad_small):
    lines, state_lines, head_part = parts
    misc = head_part + dot_nt(select_state(384, i * 384), state_lines)
    misc = misc + jnp.where(place == i, lines, 0.0)
    gains = grad_small[8:9, i * 384 : (i + 1) * 384]
    return misc + jnp.transpose(jnp.where(iota((128, 384), 0) == 24, gains, 0.0))


def backward_kernel(last, *refs):
    refs = list(refs)

    def take(n):
        taken, refs[:n] = refs[:n], []
        return taken

    (where_ref,) = take(1)
    normed_in, zx_in, ss_in, y_in, starts_in, gated_gain_in = take(6)
    weights = (take(1), take(1)) if last else (take(5), take(5))
    taps_ref, taps_state_ref, heads_ref, gain_ref = take(4)
    if last:
        dscaled_in, cot = take(2)
        stat_parts = take(4)
    else:
        chunks = take(4)
    outs = take(4 if last else 1)
    (grad_small,) = take(1)
    mine_out, theirs_out = take(2)
    normed, zx, ss, y_all, starts, gated_gain, whole, dscaled = take(8)
    x_pad, state_pad, x_conv, state_conv, du_pad, dstate_pad = take(6)
    d_hidden, d_inner, factors, sems = take(4)
    dss, products, rows_grad, sent = take(4)
    grad_taps, grad_taps_state = grad_small.at[0:8, 0:CHANNELS], grad_small.at[0:8, 768:1024]
    grad_heads, grad_gain = grad_small.at[0:8, 1024:1152], grad_small.at[8:9, :]
    copies = Copies(sems)
    place, core = where_ref[0], where_ref[1]
    if not last:
        load_out = place_blocks(copies, where_ref, weights, whole, OUT)
    load_x = copies.start(zx_in.at[:, CHANNELS:], zx.at[:, CHANNELS:])
    load_ss = copies.start(ss_in, ss)
    if last:
        load_cot = [copies.start(cot.at[k, 1], sent.at[rows_at(k), :]) for k in range(BLOCKS)]
    du_pad[SEQ:, :] = jnp.zeros((PAD, CHANNELS), F32)
    dstate_pad[SEQ:, :] = jnp.zeros((PAD, 2 * STATES), F32)
    for ref in (d_hidden, grad_small):
        ref[...] = jnp.zeros_like(ref)
    if last:
        total = stat_parts[0][...] + stat_parts[1][...] + stat_parts[2][...] + stat_parts[3][...]
        factor = lax.rsqrt(total[0:1, :] / DI + EPS)
        cubed = factor * factor * factor / DI * total[1:2, :]
        row = iota((128, SEQ), 0)
        both = jnp.where(row == 0, factor, jnp.where(row == 1, cubed, 0.0))
        for b in range(BLOCKS):
            part = slice(b * BLOCK, (b + 1) * BLOCK)
            factors[part, :] = jnp.transpose(both[:, part])
        for k in range(BLOCKS):
            rows = slice(k * BLOCK, (k + 1) * BLOCK)
            load_cot[k].wait()
            rows_grad[rows, :] = scaled_rows(sent[rows, :], factors[rows, 0:1])
    else:
        for offset, chunk in zip((0, 3, 1, 2), chunks):
            rows = rows_at(lax.rem(place + offset, 4))
            rows_grad[rows, :] = chunk[:, :D]
            tail = chunk[:, D:].astype(F32)
            factor = tail[:, 0:1] + tail[:, 1:2]
            cross = tail[:, 2:3] + tail[:, 3:4]
            lane = iota((BLOCK, 128), 1)
            cubed = factor * factor * factor / DI * cross
            factors[rows, :] = jnp.where(lane == 0, factor, jnp.where(lane == 1, cubed, 0.0))
        for load in load_out:
            load.wait()
        dscaled[...] = dot_nn(rows_grad[...], whole[:, OUT])
        rows_grad[...] = scaled_rows(rows_grad[...], factors[:, 0:1])
    load_x.wait()
    load_rows = [
        copies.start(zx_in.at[:, :CHANNELS], zx.at[:, :CHANNELS]),
        copies.start(y_in, y_all),
        copies.start(starts_in, starts),
    ]
    if last:
        load_rows.append(copies.start(dscaled_in, dscaled))
    x_pad[:PAD, :] = jnp.zeros((PAD, CHANNELS), F32)
    x_pad[PAD:, :] = zx[:, CHANNELS:]
    load_ss.wait()
    state_pad[:PAD, :] = jnp.zeros((PAD, 2 * STATES), F32)
    state_pad[PAD:, :] = ss[:, : 2 * STATES]
    conv_rows(x_pad, taps_ref, x_conv)
    conv_rows(state_pad, taps_state_ref, state_conv)
    for load in load_rows:
        load.wait()
    load_late = [
        copies.start(normed_in, normed),
        copies.start(gated_gain_in, gated_gain),
        *place_blocks(copies, where_ref, weights, whole, IN),
        *place_blocks(copies, where_ref, weights, whole, SS),
    ]

    def block(turn, carry):
        b = BLOCKS - 1 - turn
        rows = rows_at(b)
        state_u = state_conv[rows, :]
        state_s = sigmoid(state_u)
        state = state_u * state_s
        keys, reads = state[:, :STATES].astype(BF), state[:, STATES:].astype(BF)
        reads_t = jnp.transpose(state[:, STATES:]).astype(BF)
        raised, step, log_decay, summed, summed_t = step_terms(ss[rows, 2 * STATES :], heads_ref)
        meets_t = dot_nt(keys, reads)
        causal_t = iota((BLOCK, BLOCK), 1) >= iota((BLOCK, BLOCK), 0)
        fac = factors[rows, :][:, 0:1]
        cub = factors[rows, :][:, 1:2]
        d_meets_t = jnp.zeros((BLOCK, BLOCK), F32)
        d_keys = jnp.zeros((BLOCK, STATES), F32)
        d_reads = jnp.zeros((BLOCK, STATES), F32)
        head_sums = jnp.zeros((2 * BLOCK, 128), F32)
        last_row = iota((BLOCK, 128), 0) == BLOCK - 1
        for p in range(PAIRS):
            cols = slice(p * 128, (p + 1) * 128)
            u = x_conv[rows, cols]
            us = sigmoid(u)
            x = u * us
            step_wide = spread(step, 2 * p)
            summed_wide = spread(summed, 2 * p)
            grown = jnp.exp(summed_wide)
            end = grown[BLOCK - 1 : BLOCK, :]
            to_end = jnp.exp(summed_wide[BLOCK - 1 : BLOCK, :] - summed_wide)
            skip = taps_ref[6:7, cols]
            gain = taps_ref[5:6, cols]
            z = zx[rows, cols]
            zs = sigmoid(z)
            z_act = z * zs
            y = y_all[rows, cols]
            gated = y * z_act
            incoming = dscaled[rows, cols]
            lifted = gated * fac
            grad_taps[5:6, cols] += jnp.sum(incoming * lifted, axis=0, keepdims=True)
            d_gated = fac * (gain * incoming) - gated * cub
            dy = d_gated * z_act
            d_inner[rows, cols] = (d_gated * y * (zs + z_act * (1.0 - zs))).astype(BF)
            dy_low = dy.astype(BF)
            weighted = x * step_wide
            weighted_low = weighted.astype(BF)
            dy_grown = (dy * grown).astype(BF)
            held_low = starts[b, :, cols]
            dh = d_hidden[:, cols]
            dh_low = dh.astype(BF)
            d_reads = d_reads + dot_nt(dy_grown, held_low)
            kept = dot_nn(keys, dh_low) * to_end
            d_keys = d_keys + dot_nt((to_end * weighted).astype(BF), dh_low)
            decays = []
            for h in (2 * p, 2 * p + 1):
                gaps = summed_t[h : h + 1, :] - summed[:, h : h + 1]
                decays.append(jnp.exp(jnp.where(causal_t, gaps, NEG)))
            mixes = jnp.concatenate([(d * meets_t).astype(BF) for d in decays], axis=1)
            d_weighted = dot_nn(mixes, side_by_side(dy).astype(BF)) + kept
            d_mixes = dot_nt(side_by_side(weighted).astype(BF), dy_low)
            d_meets_t = d_meets_t + d_mixes[:BLOCK] * decays[0] + d_mixes[BLOCK:] * decays[1]
            dx = skip * dy + d_weighted * step_wide
            weighted_f = weighted_low.astype(F32)
            moved = dy_low.astype(F32) * (y - skip * x) - weighted_f * d_weighted
            extra = jnp.sum(weighted_f * kept, axis=0, keepdims=True) + end * jnp.sum(
                dh * held_low.astype(F32), axis=0, keepdims=True
            )
            moved = jnp.where(last_row, moved + extra, moved)
            upper, lower = two_parts(jnp.concatenate([moved, x * d_weighted], axis=0))
            picks = (
                iota((256, 128), 1) == 2 * p + (iota((256, 128), 0) % 128) // HEAD_DIM
            ).astype(BF)
            head_sums = head_sums + dot_nn(jnp.concatenate([upper, lower], axis=1), picks)
            grad_taps[6:7, cols] += jnp.sum(dy * x, axis=0, keepdims=True)
            du_pad[rows, cols] = dx * (us + x * (1.0 - us))
            d_hidden[:, cols] = end * dh + dot_nn(reads_t, dy_grown)
        d_reads = d_reads + dot_nn(jnp.transpose(d_meets_t).astype(BF), keys)
        d_keys = d_keys + dot_nn(d_meets_t.astype(BF), reads)
        d_state = jnp.concatenate([d_keys, d_reads], axis=1)
        d_state = d_state * (state_s + state * (1.0 - state_s))
        dstate_pad[rows, :] = d_state
        upper_tri = (iota((BLOCK, BLOCK), 1) >= iota((BLOCK, BLOCK), 0)).astype(F32)
        d_decay = dot_high(upper_tri, head_sums[:BLOCK])
        d_step = head_sums[BLOCK:] - d_decay * jnp.exp(heads_ref[1:2, :])
        d_raw = d_step * sigmoid(raised)
        dss[rows, 2 * STATES :] = d_raw.astype(BF)
        grad_heads[0:1, :] += jnp.sum(d_raw, axis=0, keepdims=True)
        grad_heads[1:2, :] += jnp.sum(d_decay * log_decay, axis=0, keepdims=True)
        return carry

    lax.fori_loop(0, BLOCKS, block, 0)

    def store_inner(start, cols, value):
        cols = slice(CHANNELS + cols.start, CHANNELS + cols.stop)
        d_inner[start : start + BLOCK, cols] = value

    def store_state(start, cols, value):
        dss[start : start + BLOCK, cols] = value

    conv_back(du_pad, x_pad, taps_ref, grad_taps, store_inner)
    conv_back(dstate_pad, state_pad, taps_state_ref, grad_taps_state, store_state)
    picks = (iota((CHANNELS, 128), 1) == iota((CHANNELS, 128), 0) // HEAD_DIM).astype(F32)
    grad_heads[2:3, :] = dot_high(grad_taps[...], picks)[6:7, :]
    for load in load_late:
        load.wait()
    for at in range(0, D, PART):
        cols = slice(at, at + PART)
        part = dot_nt(d_inner[...], whole[cols, IN]) + dot_nt(dss[...], whole[cols, SS])
        total = jnp.sum(part * normed[:, cols].astype(F32), axis=0, keepdims=True)
        grad_gain[:, cols] = total / gain_ref[:, cols]
        sent[:, cols] = part.astype(BF)
    if last:
        for o, out in enumerate(outs):
            copies.store(sent.at[rows_at(lax.rem(place + o, 4)), :], out)
    else:
        copies.store(sent, outs[0])
    parts = misc_parts(grad_small)
    for i in range(4):
        lanes = slice(i * 384, (i + 1) * 384)
        shared = dot_tn(normed[:, lanes], dss[...])
        for cols, value in (
            (IN, dot_tn(normed[:, lanes], d_inner[...])),
            (OUT, dot_tn(rows_grad[:, lanes], gated_gain[...])),
            (STATE, shared[:, :256]),
            (MISC, shared[:, 256:] + misc_tile(i, place, parts, grad_small)),
        ):
            low = value.astype(BF)
            for k in range(8):
                at = (4 * i + k // 2) * 48
                products[k % 2, at : at + 48, cols] = low[k * 48 : (k + 1) * 48]
        rows = slice(i * 192, (i + 1) * 192)
        copies.store(products.at[1 - core, rows, :], theirs_out.at[rows, :])
        copies.store(products.at[core, rows, :], mine_out.at[rows, :])
    copies.finish()


def backward_call(where, kept, weights, taps, taps_state, heads, gain, last, extra):
    args = [where, *kept, *weights, taps, taps_state, heads, gain, *extra]
    in_specs = [SMEM] + [HBM] * 6 + [ANY] * len(weights) + [VMEM] * 4
    in_specs += [HBM, ANY] + [VMEM] * 4 if last else [VMEM] * 4
    out_shape = [
        *([pltpu.HBM((BLOCK, D), BF)] * 4 if last else [pltpu.HBM((SEQ, D), BF)]),
        shape(16, D),
        *[pltpu.HBM((SIDE, WIDE), BF)] * 2,
    ]
    out_specs = [HBM] * (len(out_shape) - 3) + [VMEM] + [HBM] * 2
    scratch = [pltpu.VMEM(k.shape, k.dtype) for k in kept] + [pltpu.VMEM((D, WIDE), BF)]
    scratch += [
        pltpu.VMEM((SEQ, CHANNELS), F32),
        pltpu.VMEM((PAD + SEQ, CHANNELS), F32),
        pltpu.VMEM((PAD + SEQ, 2 * STATES), F32),
        pltpu.VMEM((SEQ, CHANNELS), F32),
        pltpu.VMEM((SEQ, 2 * STATES), F32),
        pltpu.VMEM((PAD + SEQ, CHANNELS), F32),
        pltpu.VMEM((PAD + SEQ, 2 * STATES), F32),
        pltpu.VMEM((STATES, CHANNELS), F32),
        pltpu.VMEM((SEQ, 2 * CHANNELS), BF),
        pltpu.VMEM((SEQ, 128), F32),
        pltpu.SemaphoreType.DMA((128,)),
        pltpu.VMEM((SEQ, 384), BF),
        pltpu.VMEM((2, SIDE, WIDE), BF),
        pltpu.VMEM((SEQ, D), BF),
        pltpu.VMEM((SEQ, D), BF),
    ]

    def kernel(*refs):
        backward_kernel(last, *refs)

    return pl.pallas_call(
        kernel,
        out_shape=out_shape,
        in_specs=in_specs,
        out_specs=out_specs,
        scratch_shapes=scratch,
        compiler_params=limit(VMEM_LIMIT),
        cost_estimate=cost(32 * 10**9, 30 * 10**6),
        name="layer_backward",
    )(*args)


def arrived(parts):
    return sum((part[...].astype(F32) for part in parts[1:]), parts[0][...].astype(F32))


def after_first_kernel(rows_ref, a, b, c, d, hidden, mixed, factor_out):
    total = arrived((a, b, c, d))
    mixed[...] = total[:, :D]
    square = total[:, D : D + 1] + total[:, D + 1 : D + 2]
    factor = lax.rsqrt(square / DI + EPS)
    factor_out[...] = jnp.broadcast_to(factor, (BLOCK, 128))
    hidden[...] = (rows_ref[...].astype(F32) + factor * total[:, :D]).astype(BF)


def after_first_call(rows, parts):
    return pl.pallas_call(
        after_first_kernel,
        out_shape=[shape(BLOCK, D, dtype=BF), shape(BLOCK, D), shape(BLOCK, 128)],
        in_specs=[VMEM] * 5,
        out_specs=[VMEM] * 3,
        name="between_layers",
    )(rows, *parts)


def after_last_kernel(where_ref, rows_ref, mixed, a, b, c, d, result):
    total = a[...] + b[...] + c[...] + d[...]
    factor = lax.rsqrt(total[0:1, :] / DI + EPS)
    row = iota((128, SEQ), 0)
    column = jnp.zeros((BLOCK, 128), F32)
    for k in range(4):
        part = slice(k * BLOCK, (k + 1) * BLOCK)
        turned = jnp.transpose(jnp.where(row[:, part] == 0, factor[:, part], 0.0))
        column = jnp.where(where_ref[0] == k, turned, column)
    result[...] = rows_ref[...].astype(F32) + column[:, 0:1] * mixed[...].astype(F32)


def after_last_call(where, rows, mixed, stat_parts):
    return pl.pallas_call(
        after_last_kernel,
        out_shape=shape(BLOCK, D),
        in_specs=[SMEM] + [VMEM] * 6,
        out_specs=VMEM,
        name="last_rows",
    )(where, rows, mixed, *stat_parts)


def rows_back(rows_ref, parts, gain_ref, grad_ref):
    incoming = arrived(parts)
    v = rows_ref[...].astype(F32)
    q = lax.rsqrt(jnp.mean(v * v, axis=1, keepdims=True) + EPS)
    weighted = incoming * gain_ref[...]
    inner = jnp.sum(weighted * v, axis=1, keepdims=True)
    return grad_ref[...].astype(F32) + q * weighted - v * (q * q * q / D * inner)


def back_last_kernel(rows_ref, a, b, c, d, gain_ref, grad_ref, mixed_ref, factor_ref, out):
    low = rows_back(rows_ref, (a, b, c, d), gain_ref, grad_ref).astype(BF)
    out[:, :D] = low
    cross = jnp.sum(low.astype(F32) * mixed_ref[...], axis=1, keepdims=True)
    factor = factor_ref[:, 0:1]
    pieces = [*two_parts(factor), *two_parts(cross)]
    lane = iota((BLOCK, 128), 1)
    tail = jnp.zeros((BLOCK, 128), F32)
    for k, piece in enumerate(pieces):
        tail = jnp.where(lane == k, piece.astype(F32), tail)
    out[:, D:] = tail.astype(BF)


def back_last_call(rows, parts, gain, grad, mixed, factor):
    return pl.pallas_call(
        back_last_kernel,
        out_shape=shape(BLOCK, SENT, dtype=BF),
        in_specs=[VMEM] * 9,
        out_specs=VMEM,
        name="between_layers_back",
    )(rows, *parts, gain, grad, mixed, factor)


def back_first_kernel(rows_ref, incoming, gain_ref, grad_ref, out):
    out[...] = rows_back(rows_ref, (incoming,), gain_ref, grad_ref[:, :D])


def back_first_call(rows, incoming, gain, grad):
    return pl.pallas_call(
        back_first_kernel,
        out_shape=shape(BLOCK, D),
        in_specs=[VMEM] * 4,
        out_specs=VMEM,
        name="first_rows_back",
    )(rows, incoming, gain, grad)


def params_kernel(where_ref, misc, heads_ref, taps, taps_state, gain):
    small_params(where_ref[0], misc, heads_ref, taps, taps_state, gain)


def params_call(where, misc, heads):
    return pl.pallas_call(
        params_kernel,
        out_shape=SMALL,
        in_specs=[SMEM, VMEM, VMEM],
        out_specs=[VMEM] * 3,
        compiler_params=limit(16),
        name="small_parameters",
    )(where, misc, heads)


def both_kernel(where_ref, mine, given, *outs):
    if len(outs) == 1:
        outs[0][...] = (mine[...].astype(F32) + given[...].astype(F32)).astype(BF)
        return
    core, row, col = where_ref[1], where_ref[2], where_ref[3]
    own, ahead, far_left, far_right, behind, parts = outs
    for i in range(4):
        for j in range(4):
            rows = slice((4 * i + j) * 48, (4 * i + j + 1) * 48)
            total = (mine[rows, :].astype(F32) + given[rows, :].astype(F32)).astype(BF)
            along, across = lax.rem(i - row + 4, 4), lax.rem(j - col + 4, 4)
            o = along + core * (across - along)
            q = across + core * (along - across)
            parts[o, pl.ds(pl.multiple_of(q * 48, 16), 48), :] = total
    own[...] = parts[0]
    ahead[...] = parts[1]
    far_left[...] = parts[2, :, LEFT]
    far_right[...] = parts[2, :, RIGHT]
    behind[...] = parts[3]


def ring_shapes(rows):
    whole = shape(rows, WIDE, dtype=BF)
    left, right = shape(rows, SPLIT, dtype=BF), shape(rows, WIDE - SPLIT, dtype=BF)
    return [whole, whole, left, right, whole]


def both_call(where, mine, given, relative):
    out_shape = ring_shapes(192) if relative else [shape(SIDE, WIDE, dtype=BF)]
    return pl.pallas_call(
        both_kernel,
        out_shape=out_shape,
        in_specs=[SMEM] + [VMEM] * 2,
        out_specs=[VMEM] * len(out_shape),
        scratch_shapes=[pltpu.VMEM((4, 192, WIDE), BF)] if relative else [],
        compiler_params=limit(28),
        cost_estimate=cost(10**6, 10**4),
        name="both_cores_grads",
    )(where, mine, given)


def passed_kernel(ahead, behind, left, right, out_ahead, out_behind):
    out_ahead[:, LEFT] = (ahead[:, LEFT].astype(F32) + left[...].astype(F32)).astype(BF)
    out_ahead[:, RIGHT] = ahead[:, RIGHT]
    out_behind[:, LEFT] = behind[:, LEFT]
    out_behind[:, RIGHT] = (behind[:, RIGHT].astype(F32) + right[...].astype(F32)).astype(BF)


def passed_call(ahead, behind, left, right):
    return pl.pallas_call(
        passed_kernel,
        out_shape=[shape(*ahead.shape, dtype=BF)] * 2,
        in_specs=[VMEM] * 4,
        out_specs=[VMEM] * 2,
        compiler_params=limit(16),
        cost_estimate=cost(10**6, 10**4),
        name="grads_passed_on",
    )(ahead, behind, left, right)


def halfway_kernel(a, b, c, own, ahead, far_left, far_right, behind):
    total = arrived((a, b, c)).astype(BF)
    own[...] = total[:48]
    ahead[...] = total[48:96]
    far_left[...] = total[96:144, LEFT]
    far_right[...] = total[96:144, RIGHT]
    behind[...] = total[144:]


def halfway_call(parts):
    return pl.pallas_call(
        halfway_kernel,
        out_shape=ring_shapes(48),
        in_specs=[VMEM] * 3,
        out_specs=[VMEM] * 5,
        compiler_params=limit(20),
        name="grads_halfway",
    )(*parts)


def shard_kernel(where_ref, a, b, c, share_1, own, given):
    share_0 = arrived((a, b, c))
    is_first = where_ref[1] == 0
    other = share_1[...].astype(F32)
    own[...] = jnp.where(is_first, share_0, other)
    given[...] = jnp.where(is_first, other, share_0).astype(BF)


def shard_call(where, parts, share_1):
    return pl.pallas_call(
        shard_kernel,
        out_shape=[shape(48, WIDE), shape(48, WIDE, dtype=BF)],
        in_specs=[SMEM] + [VMEM] * 4,
        out_specs=[VMEM] * 2,
        name="grads_shard",
    )(where, *parts, share_1)


def swap(v):
    return lax.ppermute(v, "section", [(0, 1), (1, 0)])


def turn(v, by, axis="tensor"):
    return lax.ppermute(v, axis, [(i, (i + by) % 4) for i in range(4)])


def spread_rows(v):
    return (v, turn(v, 1), turn(v, -1), turn(v, 2))


def meet(parts, axis="tensor"):
    own, ahead, across, behind = parts
    return (own, turn(ahead, 1, axis), turn(behind, -1, axis), turn(across, 2, axis))


def from_ring(v, axis):
    return (v, turn(v, -1, axis), turn(v, 2, axis), turn(v, 1, axis))


def ring(v, by, phase):
    pairs = []
    for s in range(2):
        for a in range(4):
            for b in range(4):
                to = ((a + by) % 4, b) if s == phase else (a, (b + by) % 4)
                pairs.append((16 * s + 4 * a + b, 16 * s + 4 * to[0] + to[1]))
    return lax.ppermute(v, ("section", *DP), pairs)


def around(v, phase):
    ahead, behind = lax.optimization_barrier((ring(v, -1, phase), ring(v, 1, phase)))
    return (
        v,
        ahead,
        ring(ahead[:, :SPLIT], -1, phase),
        ring(behind[:, SPLIT:], 1, phase),
        behind,
    )


def gather_by_turns(main, rest):
    own, ahead, far_left, far_right, behind = around(main, 0)
    far = jnp.concatenate([far_left, far_right], axis=1)
    rest = (rest, ring(rest, -1, 0), ring(rest, 2, 0), ring(rest, 1, 0))
    rows = [
        jnp.concatenate(pair, axis=1) for pair in zip((own, ahead, far, behind), rest)
    ]
    return around(jnp.concatenate(rows, axis=0), 1)


def pick(v, index, axis):
    return lax.dynamic_index_in_dim(v, index, axis, keepdims=False)


def tie(*values):
    return lax.optimization_barrier(values)


def shards(
    section_ends,
    norm_gain,
    proj_inner,
    proj_step,
    proj_state,
    conv_inner,
    conv_state,
    gate_gain,
    head_params,
    proj_output,
):
    core = lax.axis_index("section")
    place = lax.axis_index("tensor")
    is_first = core == 0
    where = jnp.stack(
        [place, core, lax.axis_index("dp_0"), lax.axis_index("dp_1")]
    ).astype(jnp.int32)

    packed = jnp.concatenate(
        [
            proj_state[0].reshape(-1),
            norm_gain[0],
            conv_inner[0].reshape(-1),
            gate_gain[0],
            conv_state[0].reshape(-1),
            jnp.zeros((32 * 256 - 6144 - 332,), BF),
        ]
    ).reshape(32, 256)
    turned = jnp.stack(from_ring(packed, "tensor") * 2)
    filled = lax.dynamic_slice_in_dim(turned, lax.rem(4 - place, 4), 4, 0).reshape(4, 32 * 256)
    state_rows = filled[:, :6144].reshape(96, 256)
    norm_col = filled[:, 6144:6168].reshape(96, 1)
    inner_cols = filled[:, 6168:6408].reshape(4, 5, 48).transpose(0, 2, 1).reshape(192, 5)
    gate_col = filled[:, 6408:6456].reshape(192, 1)
    both = jnp.concatenate([inner_cols, gate_col], axis=1)
    both = both.reshape(2, 96, 6).transpose(1, 0, 2).reshape(96, 12)
    state_cols = filled[:, 6456:6476].reshape(4, 5, 4).transpose(0, 2, 1).reshape(16, 5)
    state_cols = jnp.pad(state_cols, ((0, 80), (0, 0)))
    misc = jnp.concatenate(
        [proj_step[0], both, norm_col, state_cols, jnp.zeros((96, 128 - 30), BF)], axis=1
    )

    def by_layer_of(keep, got):
        return jnp.where(is_first, keep, got), jnp.where(is_first, got, keep)

    def by_layer(halves):
        return by_layer_of(pick(halves, core, 0), swap(pick(halves, 1 - core, 0)))

    main = jnp.concatenate([proj_inner[0].reshape(96, 2 * CHANNELS), proj_output[0].T], axis=1)
    main_0, main_1 = by_layer(main.reshape(2, 48, MAIN))
    main_0, heads_got = tie(main_0, swap(head_params[0]))
    rest_0, rest_1 = by_layer(jnp.concatenate([state_rows, misc], axis=1).reshape(2, 48, 384))

    ends = section_ends[0]
    got_rows = swap(pick(ends, 1 - core, 0))
    rows_in = jnp.where(is_first, ends[0], got_rows)
    cot = jnp.where(is_first, got_rows, ends[1])
    heads = [
        jnp.pad(v.astype(F32), ((0, 5), (0, 128 - HEADS)))
        for v in by_layer_of(head_params[0], heads_got)
    ]
    ends_all = lax.all_gather(jnp.stack([rows_in, cot]), "tensor", axis=0)
    own_pieces = gather_by_turns(main_0, rest_0)
    shard_1 = jnp.concatenate([main_1, rest_1], axis=1)
    shard_1, *rest = tie(shard_1, *heads, *own_pieces)
    heads, own_pieces = rest[:2], rest[2:]
    full_1 = lax.all_gather(shard_1, DP, axis=0, tiled=True)
    pieces_0 = (*own_pieces, *[swap(v) for v in own_pieces])
    first = forward_call(where, ends_all, (), (*pieces_0, heads[0]))
    kept_0, sent_0, small_0 = first[:6], first[6:10], first[10:]
    weights_0 = (pieces_0, small_0[0], small_0[1], heads[0], small_0[2])
    own_1, *met_0 = tie(full_1, *meet(sent_0))
    other_1 = swap(own_1)
    order = (own_1[:, MISC].reshape(16, 48, 128), other_1[:, MISC].reshape(16, 48, 128))
    misc_1 = jnp.where(is_first, jnp.stack(order, axis=1), jnp.stack(order[::-1], axis=1))
    small_1 = params_call(where, misc_1.reshape(D, 128), heads[1])
    weights_1 = ((own_1, other_1), small_1[0], small_1[1], heads[1], small_1[2])
    hidden, mixed_0, factor_0 = after_first_call(rows_in, met_0)
    kept_1 = forward_call(
        where, ends_all, spread_rows(hidden), (own_1, other_1, *weights_1[1:])
    )
    dscaled_1, stats, mixed_1 = kept_1[6:]
    stat_parts = spread_rows(stats)
    met_1 = lax.psum_scatter(mixed_1, "tensor", scatter_dimension=0, tiled=True)
    back_1 = backward_call(
        where, kept_1[:6], *weights_1, True, (dscaled_1, ends_all, *stat_parts)
    )
    met_1, *back_1 = tie(met_1, *back_1)
    payload_1 = both_call(where, back_1[5], swap(back_1[6]), False)[0]
    payload_1, *d_met_1 = tie(payload_1, *meet(back_1[:4]))
    grad_1 = back_last_call(hidden, d_met_1, weights_1[4], cot, mixed_0, factor_0)
    payload_1, met_1, grad_1 = tie(payload_1, met_1, grad_1)
    share_1 = lax.psum_scatter(payload_1, DP, scatter_dimension=0, tiled=True)
    result = after_last_call(where, hidden, met_1, stat_parts)
    result, *chunks_0 = tie(result, *spread_rows(grad_1))
    back_0 = backward_call(where, kept_0, *weights_0, False, chunks_0)
    parts_0 = both_call(where, back_0[2], swap(back_0[3]), True)
    own, ahead, far_left, far_right, behind = parts_0
    ahead, behind = passed_call(
        ahead, behind, ring(far_left, 1, 0), ring(far_right, -1, 0)
    )
    share_1, rows_0, ahead, behind = tie(share_1, back_0[0], ahead, behind)
    ahead, behind = tie(ring(ahead, 1, 0), ring(behind, -1, 0))
    pieces = halfway_call((own, ahead, behind))
    met_0 = lax.psum_scatter(rows_0, "tensor", scatter_dimension=0, tiled=True)
    own, ahead, far_left, far_right, behind = pieces
    ahead, behind = passed_call(
        ahead, behind, ring(far_left, 1, 1), ring(far_right, -1, 1)
    )
    met_0, ahead, behind = tie(met_0, ahead, behind)
    half_met = (own, ring(ahead, 1, 1), ring(behind, -1, 1))
    grad_0 = back_first_call(rows_in, met_0, weights_0[4], grad_1)
    rows_got = swap(jnp.where(is_first, result, grad_0))
    section_rows = jnp.where(
        is_first, jnp.stack([grad_0, rows_got]), jnp.stack([rows_got, result])
    )
    share_own, share_given = shard_call(where, half_met, share_1)
    share_got = swap(share_given).astype(F32)
    whole = jnp.where(
        is_first,
        jnp.concatenate([share_own, share_got], axis=0),
        jnp.concatenate([share_got, share_own], axis=0),
    )
    grad_inner = whole[:, IN].reshape(96, 2, CHANNELS)
    grad_output = whole[:, OUT].T
    misc = whole[:, MISC]
    grad_step = misc[:, :HEADS]
    grad_heads = misc[:HEADS, 30:33].T
    to_send = jnp.concatenate(
        [
            whole[:, STATE].reshape(4, 6144),
            misc[:, 24].reshape(4, 24),
            misc[:, 12:24].reshape(96, 2, 6).transpose(1, 0, 2).reshape(4, 48 * 6),
            misc[:16, 25:30].reshape(4, 20),
            jnp.zeros((4, 32 * 256 - 6144 - 332), F32),
        ],
        axis=1,
    ).reshape(4, 32, 256)
    pieces = [pick(to_send, lax.rem(place + o, 4), 0) for o in range(4)]
    section_rows, *met = tie(section_rows, *meet(pieces))
    total = (met[0] + met[1] + met[2] + met[3]).reshape(-1)
    grad_state = total[:6144].reshape(24, 256)
    grad_norm = total[6144:6168]
    inner_lines = total[6168:6456].reshape(48, 6).T
    grad_conv_inner = inner_lines[:5]
    grad_gate = inner_lines[5]
    grad_conv_state = total[6456:6476].reshape(4, 5).T
    return (
        section_rows[None],
        grad_norm[None],
        grad_inner[None],
        grad_step[None],
        grad_state[None],
        grad_conv_inner[None],
        grad_conv_state[None],
        grad_gate[None],
        grad_heads[None],
        grad_output[None],
    )


def solution(mesh):
    split = Mesh(
        mesh.devices.reshape(mesh.shape["section"], 4, 4, mesh.shape["tensor"]),
        ("section", "dp_0", "dp_1", "tensor"),
    )
    return jax.shard_map(
        shards,
        mesh=split,
        in_specs=(
            P("section", None, DP_TENSOR, None),
            P("section", DP_TENSOR),
            P("section", DP, None, "tensor"),
            P("section", DP, "tensor"),
            P("section", DP_TENSOR, None),
            P("section", None, DP_TENSOR),
            P("section", None, DP_TENSOR),
            P("section", DP_TENSOR),
            P("section", None, "tensor"),
            P("section", "tensor", DP),
        ),
        out_specs=(
            P("section", None, DP_TENSOR, None),
            P("section", DP_TENSOR),
            P("section", DP, None, "tensor"),
            P("section", DP, "tensor"),
            P("section", DP_TENSOR, None),
            P("section", None, DP_TENSOR),
            P("section", None, DP_TENSOR),
            P("section", DP_TENSOR),
            P("section", None, "tensor"),
            P("section", "tensor", DP),
        ),
        check_vma=False,
    )
```

profile of v0, /device:TPU:0, one launch (start us, length us, event | category | flops | bytes accessed | tf_op | source)
XLA Modules:
  0.0 372.7 jit_solution(3929425771107060680)
XLA Ops:
  11.1 4.2 %collective-permute-start.2 = (bf16[32,256]{1,0:T(8,128)(2,1)S(1)}, bf16[32,256]{1,0:T(8,128)(2,1)S(1)}, u32[]{:S(2)}, u32[]{:S(2)}) collective-permute-start(bf16[32,256]{1,0:T(8,128)(2,1)S(1)} %reshape.97), channel_id=1, source_target_pairs={{0,3},{1,0},{2,1},{3,2},{4,7},{5,4},{6,5},{7,6},{8,11},{9,8},{10,9... | collective-permute-start | bytes 49160 | tf_op jit(solution)/shard_map/ppermute | solution.py:941
  22.7 3.1 collective-permute-start.7
  29.2 3.7 collective-permute-done.8
  33.0 3.3 collective-permute-start.10
  42.9 3.0 collective-permute-start.14
  45.8 12.1 %collective-permute-done.14.refs_3_.refs_8_ = bf16[192,2688]{1,0:T(8,128)(2,1)S(1)} collective-permute-done((bf16[192,2688]{1,0:T(8,128)(2,1)S(1)}, bf16[192,2688]{1,0:T(8,128)(2,1)S(1)}, u32[]{:S(2)}, u32[]{:S(2)}) %collective-permute-start.14) | collective-permute-done | bytes 1032224 | tf_op jit(solution)/shard_map/ppermute | solution.py:964
  58.0 3.7 collective-permute-done.15.refs_6_.refs_11_
  65.3 6.5 %collective-permute-done.17.refs_5_.refs_10_ = bf16[192,1152]{1,0:T(8,128)(2,1)} collective-permute-done((bf16[192,1152]{1,0:T(8,128)(2,1)S(1)}, bf16[192,1152]{1,0:T(8,128)(2,1)}, u32[]{:S(2)}, u32[]{:S(2)}) %collective-permute-start.17) | collective-permute-done | bytes 442400 | tf_op jit(solution)/shard_map/ppermute | solution.py:964
  73.8 5.6 %collective-permute-done.21.refs_10_.refs_15_ = bf16[192,1152]{1,0:T(8,128)(2,1)} collective-permute-done((bf16[192,1152]{1,0:T(8,128)(2,1)}, bf16[192,1152]{1,0:T(8,128)(2,1)}, u32[]{:S(2)}, u32[]{:S(2)}) %collective-permute-start.21) | collective-permute-done | bytes 442400 | tf_op jit(solution)/shard_map/ppermute | solution.py:937
  80.3 17.1 %layer_forward.2 = (bf16[512,1536]{1,0:T(8,128)(2,1)}, f32[512,1536]{1,0:T(8,128)}, f32[512,384]{1,0:T(8,128)}, f32[512,768]{1,0:T(8,128)}, bf16[4,128,768]{2,1,...) custom-call(s32[4]{0:T(128)} %pad_add_fusion.refs_0_.where_ref, ...), custom_call_target="tpu_custom_call" | custom-call | flops 20000000000 | bytes 24000000 | tf_op jit(solution)/shard_map/layer_forward/pallas_call | solution.py:424
  97.4 2.7 collective-permute-start.23
  102.2 9.1 %collective-permute-done.23.b = bf16[128,1664]{1,0:T(8,128)(2,1)S(1)} collective-permute-done((bf16[128,1664]{1,0:T(8,128)(2,1)}, bf16[128,1664]{1,0:T(8,128)(2,1)S(1)}, u32[]{:S(2)}, u32[]{:S(2)}) %collective-permute-start.23) | collective-permute-done | bytes 426016 | tf_op jit(solution)/shard_map/ppermute | solution.py:941
  112.9 7.2 %collective-permute-done.25.d = bf16[128,1664]{1,0:T(8,128)(2,1)S(1)} collective-permute-done((bf16[128,1664]{1,0:T(8,128)(2,1)}, bf16[128,1664]{1,0:T(8,128)(2,1)S(1)}, u32[]{:S(2)}, u32[]{:S(2)}) %collective-permute-start.25) | collective-permute-done | bytes 426016 | tf_op jit(solution)/shard_map/ppermute | solution.py:941
  121.0 2.9 between_layers.1
  137.6 8.8 %collective-permute-done.28.refs_5_ = bf16[128,1536]{1,0:T(8,128)(2,1)S(1)} collective-permute-done((bf16[128,1536]{1,0:T(8,128)(2,1)}, bf16[128,1536]{1,0:T(8,128)(2,1)S(1)}, u32[]{:S(2)}, u32[]{:S(2)}) %collective-permute-start.28) | collective-permute-done | bytes 393248 | tf_op jit(solution)/shard_map/ppermute | solution.py:941
  147.2 20.1 %layer_forward.3 = (bf16[512,1536]{1,0:T(8,128)(2,1)}, f32[512,1536]{1,0:T(8,128)}, f32[512,384]{1,0:T(8,128)}, f32[512,768]{1,0:T(8,128)}, bf16[4,128,768]{2,1,...) custom-call(s32[4]{0:T(128)} %pad_add_fusion.refs_0_.where_ref, ...), custom_call_target="tpu_custom_call" | custom-call | flops 20000000000 | bytes 24000000 | tf_op jit(solution)/shard_map/layer_forward/pallas_call | solution.py:424
  172.7 3.5 collective-permute-done.32.refs_18_.d
  176.8 29.6 %layer_backward.2 = (bf16[128,1536]{1,0:T(8,128)(2,1)}, bf16[128,1536]{1,0:T(8,128)(2,1)}, bf16[128,1536]{1,0:T(8,128)(2,1)}, bf16[128,1536]{1,0:T(8,128)(2,1)},...) custom-call(s32[4]{0:T(128)} %pad_add_fusion.refs_0_.where_ref, ...), custom_call_target="tpu_custom_call" | custom-call | flops 32000000000 | bytes 30000000 | tf_op jit(solution)/shard_map/layer_backward/pallas_call | solution.py:720
  206.6 3.2 collective-permute-start.35
  210.0 3.8 %collective-permute-done.33.given = bf16[768,2688]{1,0:T(8,128)(2,1)S(1)} collective-permute-done((bf16[768,2688]{1,0:T(8,128)(2,1)}, bf16[768,2688]{1,0:T(8,128)(2,1)S(1)}, u32[]{:S(2)}, u32[]{:S(2)}) %collective-permute-start.33) | collective-permute-done | bytes 4128800 | tf_op jit(solution)/shard_map/ppermute | solution.py:937
  219.4 8.4 %collective-permute-done.34.b = bf16[128,1536]{1,0:T(8,128)(2,1)S(1)} collective-permute-done((bf16[128,1536]{1,0:T(8,128)(2,1)}, bf16[128,1536]{1,0:T(8,128)(2,1)S(1)}, u32[]{:S(2)}, u32[]{:S(2)}) %collective-permute-start.34) | collective-permute-done | bytes 393248 | tf_op jit(solution)/shard_map/ppermute | solution.py:941
  228.9 3.3 between_layers_back.1.refs_21_.grad_ref
  233.8 2.6 collective-permute-start.38
  239.8 6.9 %collective-permute-done.37.refs_22_ = bf16[128,1664]{1,0:T(8,128)(2,1)S(1)} collective-permute-done((bf16[128,1664]{1,0:T(8,128)(2,1)S(1)}, bf16[128,1664]{1,0:T(8,128)(2,1)S(1)}, u32[]{:S(2)}, u32[]{:S(2)}) %collective-permute-start.37) | collective-permute-done | bytes 426016 | tf_op jit(solution)/shard_map/ppermute | solution.py:941
  246.7 7.5 %collective-permute-done.38.refs_23_ = bf16[128,1664]{1,0:T(8,128)(2,1)S(1)} collective-permute-done((bf16[128,1664]{1,0:T(8,128)(2,1)S(1)}, bf16[128,1664]{1,0:T(8,128)(2,1)S(1)}, u32[]{:S(2)}, u32[]{:S(2)}) %collective-permute-start.38) | collective-permute-done | bytes 426016 | tf_op jit(solution)/shard_map/ppermute | solution.py:941
  256.4 31.0 %layer_backward.3 = (bf16[512,1536]{1,0:T(8,128)(2,1)}, f32[16,1536]{1,0:T(8,128)}, bf16[768,2688]{1,0:T(8,128)(2,1)}, bf16[768,2688]{1,0:T(8,128)(2,1)}) custom-call(s32[4]{0:T(128)} %pad_add_fusion.refs_0_.where_ref, bf16[512,1536]{1,0:T(8,128)(2,1)} %get-tuple-element.173.refs_1_, f32[512,1536]{1,0:T(8,128)} %get-tuple-element.174.refs_2_, ...), custom_call_target="tpu_custom_call" | custom-call | flops 32000000000 | bytes 30000000 | tf_op jit(solution)/shard_map/layer_backward/pallas_call | solution.py:720
  287.7 7.3 %collective-permute-done.40.given = bf16[768,2688]{1,0:T(8,128)(2,1)S(1)} collective-permute-done((bf16[768,2688]{1,0:T(8,128)(2,1)}, bf16[768,2688]{1,0:T(8,128)(2,1)S(1)}, u32[]{:S(2)}, u32[]{:S(2)}) %collective-permute-start.40) | collective-permute-done | bytes 4128800 | tf_op jit(solution)/shard_map/ppermute | solution.py:937
  303.2 7.8 %collective-permute-done.42.right = bf16[192,1152]{1,0:T(8,128)(2,1)S(1)} collective-permute-done((bf16[192,1152]{1,0:T(8,128)(2,1)S(1)}, bf16[192,1152]{1,0:T(8,128)(2,1)S(1)}, u32[]{:S(2)}, u32[]{:S(2)}) %collective-permute-start.42) | collective-permute-done | bytes 442400 | tf_op jit(solution)/shard_map/ppermute | solution.py:964
  313.5 3.2 collective-permute-start.44
  316.7 12.6 %collective-permute-done.43.b = bf16[192,2688]{1,0:T(8,128)(2,1)S(1)} collective-permute-done((bf16[192,2688]{1,0:T(8,128)(2,1)S(1)}, bf16[192,2688]{1,0:T(8,128)(2,1)S(1)}, u32[]{:S(2)}, u32[]{:S(2)}) %collective-permute-start.43) | collective-permute-done | bytes 1032224 | tf_op jit(solution)/shard_map/ppermute | solution.py:964
  353.0 2.9 collective-permute-start.52
  359.6 2.7 maximum_select_fusion
  (287 shorter events, 108.3 us)
Async XLA Ops:
  7.2 72.2 %all-gather.6.cloned.1.call-start = ((), (), s32[]{:S(2)}) async-start(), calls=%async_computation.6 | async-start | bytes 3932160 | tf_op jit(solution)/shard_map/all_gather | solution.py:1058
  11.1 10.7 %collective-permute-start.2 = (bf16[32,256]{1,0:T(8,128)(2,1)S(1)}, bf16[32,256]{1,0:T(8,128)(2,1)S(1)}, u32[]{:S(2)}, u32[]{:S(2)}) collective-permute-start(bf16[32,256]{1,0:T(8,128)(2,1)S(1)} %reshape.97), channel_id=1, source_target_pairs={{0,3},{1,0},{2,1},{3,2},{4,7},{5,4},{6,5},{7,6},{8,11},{9,8},{10,9... | collective-permute-start | bytes 49160 | tf_op jit(solution)/shard_map/ppermute | solution.py:941
  21.8 99.2 %all-gather.4.cloned.1.call-start = ((), (), s32[]{:S(2)}) async-start(), calls=%async_computation.3 | async-start | bytes 4386816 | tf_op jit(solution)/shard_map/all_gather | solution.py:1063
  26.5 9.8 %collective-permute-start.5 = (bf16[48,384]{1,0:T(8,128)(2,1)S(1)}, bf16[48,384]{1,0:T(8,128)(2,1)S(1)}, u32[]{:S(2)}, u32[]{:S(2)}) collective-permute-start(bf16[48,384]{1,0:T(8,128)(2,1)S(1)} %dynamic-slice_bitcast_fusion.2), channel_id=1, source_target_pairs={{0,64},{64,0},{1,65},{65,1},{2,66},{66,2},{3,67},{67,3},{4,68},{68... | collective-permute-start | bytes 110600 | tf_op jit(solution)/shard_map/ppermute | solution.py:937
  32.9 9.8 %collective-permute-start.11 = (bf16[48,768]{1,0:T(8,128)(2,1)S(1)}, bf16[48,768]{1,0:T(8,128)(2,1)S(1)}, u32[]{:S(2)}, u32[]{:S(2)}) collective-permute-start(bf16[48,768]{1,0:T(8,128)(2,1)S(1)} %slice.98), channel_id=1, source_target_pairs={{0,16},{4,20},{8,24},{12,28},{16,32},{20,36},{24,40},{28,44},{32,4... | collective-permute-start | bytes 221192 | tf_op jit(solution)/shard_map/ppermute | solution.py:964
  33.0 9.8 %collective-permute-start.10 = (bf16[48,1536]{1,0:T(8,128)(2,1)S(1)}, bf16[48,1536]{1,0:T(8,128)(2,1)S(1)}, u32[]{:S(2)}, u32[]{:S(2)}) collective-permute-start(bf16[48,1536]{1,0:T(8,128)(2,1)S(1)} %slice.97), channel_id=1, source_target_pairs={{0,48},{4,52},{8,56},{12,60},{16,0},{20,4},{24,8},{28,12},{32,16},... | collective-permute-start | bytes 442376 | tf_op jit(solution)/shard_map/ppermute | solution.py:964
  42.9 15.1 %collective-permute-start.14 = (bf16[192,2688]{1,0:T(8,128)(2,1)S(1)}, bf16[192,2688]{1,0:T(8,128)(2,1)S(1)}, u32[]{:S(2)}, u32[]{:S(2)}) collective-permute-start(bf16[192,2688]{1,0:T(8,128)(2,1)S(1)} %maximum_maximum_fusion.refs_2_.refs_7_), channel_id=1, source_target_pairs={{0,12},{4,0},{8,4},{12,8},{16,28},{20,16},{24,20},{28,24},{32,44},... | collective-permute-start | bytes 3096584 | tf_op jit(solution)/shard_map/ppermute | solution.py:964
  45.8 15.8 %collective-permute-start.15 = (bf16[192,2688]{1,0:T(8,128)(2,1)S(1)}, bf16[192,2688]{1,0:T(8,128)(2,1)S(1)}, u32[]{:S(2)}, u32[]{:S(2)}) collective-permute-start(bf16[192,2688]{1,0:T(8,128)(2,1)S(1)} %maximum_maximum_fusion.refs_2_.refs_7_), channel_id=1, source_target_pairs={{0,4},{4,8},{8,12},{12,0},{16,20},{20,24},{24,28},{28,16},{32,36},... | collective-permute-start | bytes 3096584 | tf_op jit(solution)/shard_map/ppermute | solution.py:964
  61.7 10.1 %collective-permute-start.16 = (bf16[192,1536]{1,0:T(8,128)(2,1)S(1)}, bf16[192,1536]{1,0:T(8,128)(2,1)}, u32[]{:S(2)}, u32[]{:S(2)}) collective-permute-start(bf16[192,1536]{1,0:T(8,128)(2,1)S(1)} %slice.99), channel_id=1, source_target_pairs={{0,12},{4,0},{8,4},{12,8},{16,28},{20,16},{24,20},{28,24},{32,44},... | collective-permute-start | bytes 1769480 | tf_op jit(solution)/shard_map/ppermute | solution.py:964
  62.0 9.7 %collective-permute-start.17 = (bf16[192,1152]{1,0:T(8,128)(2,1)S(1)}, bf16[192,1152]{1,0:T(8,128)(2,1)}, u32[]{:S(2)}, u32[]{:S(2)}) collective-permute-start(bf16[192,1152]{1,0:T(8,128)(2,1)S(1)} %slice.100), channel_id=1, source_target_pairs={{0,4},{4,8},{8,12},{12,0},{16,20},{20,24},{24,28},{28,16},{32,36},... | collective-permute-start | bytes 1327112 | tf_op jit(solution)/shard_map/ppermute | solution.py:964
  71.8 134.6 %reduce-scatter.6.cloned.1.call-start = ((), (), s32[]{:S(2)}) async-start(), calls=%async_computation.4 | async-start | bytes 1966080 | tf_op jit(solution)/shard_map/reduce_scatter | solution.py:1080
  97.4 13.9 %collective-permute-start.23 = (bf16[128,1664]{1,0:T(8,128)(2,1)}, bf16[128,1664]{1,0:T(8,128)(2,1)S(1)}, u32[]{:S(2)}, u32[]{:S(2)}) collective-permute-start(bf16[128,1664]{1,0:T(8,128)(2,1)} %get-tuple-element.130), channel_id=1, source_target_pairs={{0,1},{1,2},{2,3},{3,0},{4,5},{5,6},{6,7},{7,4},{8,9},{9,10},{10,1... | collective-permute-start | bytes 1277960 | tf_op jit(solution)/shard_map/ppermute | solution.py:941
  100.0 12.9 %collective-permute-start.24 = (bf16[128,1664]{1,0:T(8,128)(2,1)}, bf16[128,1664]{1,0:T(8,128)(2,1)S(1)}, u32[]{:S(2)}, u32[]{:S(2)}) collective-permute-start(bf16[128,1664]{1,0:T(8,128)(2,1)} %get-tuple-element.131), channel_id=1, source_target_pairs={{0,3},{1,0},{2,1},{3,2},{4,7},{5,4},{6,5},{7,6},{8,11},{9,8},{10,9... | collective-permute-start | bytes 1277960 | tf_op jit(solution)/shard_map/ppermute | solution.py:941
  100.7 19.5 %collective-permute-start.25 = (bf16[128,1664]{1,0:T(8,128)(2,1)}, bf16[128,1664]{1,0:T(8,128)(2,1)S(1)}, u32[]{:S(2)}, u32[]{:S(2)}) collective-permute-start(bf16[128,1664]{1,0:T(8,128)(2,1)} %get-tuple-element.132), channel_id=1, source_target_pairs={{0,2},{1,3},{2,0},{3,1},{4,6},{5,7},{6,4},{7,5},{8,10},{9,11},{10,... | collective-permute-start | bytes 1277960 | tf_op jit(solution)/shard_map/ppermute | solution.py:941
  123.9 12.9 %collective-permute-start.26 = (bf16[128,1536]{1,0:T(8,128)(2,1)}, bf16[128,1536]{1,0:T(8,128)(2,1)S(1)}, u32[]{:S(2)}, u32[]{:S(2)}) collective-permute-start(bf16[128,1536]{1,0:T(8,128)(2,1)} %get-tuple-element.137.refs_2_.rows_ref), channel_id=1, source_target_pairs={{0,1},{1,2},{2,3},{3,0},{4,5},{5,6},{6,7},{7,4},{8,9},{9,10},{10,1... | collective-permute-start | bytes 1179656 | tf_op jit(solution)/shard_map/ppermute | solution.py:941
  125.4 12.2 %collective-permute-start.27 = (bf16[128,1536]{1,0:T(8,128)(2,1)}, bf16[128,1536]{1,0:T(8,128)(2,1)S(1)}, u32[]{:S(2)}, u32[]{:S(2)}) collective-permute-start(bf16[128,1536]{1,0:T(8,128)(2,1)} %get-tuple-element.137.refs_2_.rows_ref), channel_id=1, source_target_pairs={{0,3},{1,0},{2,1},{3,2},{4,7},{5,4},{6,5},{7,6},{8,11},{9,8},{10,9... | collective-permute-start | bytes 1179656 | tf_op jit(solution)/shard_map/ppermute | solution.py:941
  127.3 19.1 %collective-permute-start.28 = (bf16[128,1536]{1,0:T(8,128)(2,1)}, bf16[128,1536]{1,0:T(8,128)(2,1)S(1)}, u32[]{:S(2)}, u32[]{:S(2)}) collective-permute-start(bf16[128,1536]{1,0:T(8,128)(2,1)} %get-tuple-element.137.refs_2_.rows_ref), channel_id=1, source_target_pairs={{0,2},{1,3},{2,0},{3,1},{4,6},{5,7},{6,4},{7,5},{8,10},{9,11},{10,... | collective-permute-start | bytes 1179656 | tf_op jit(solution)/shard_map/ppermute | solution.py:941
  167.4 146.0 %reduce-scatter.10.cloned.1.call-start = ((), (), s32[]{:S(2)}) async-start(), calls=%async_computation.7 | async-start | bytes 4386816
  206.5 21.4 %collective-permute-start.34 = (bf16[128,1536]{1,0:T(8,128)(2,1)}, bf16[128,1536]{1,0:T(8,128)(2,1)S(1)}, u32[]{:S(2)}, u32[]{:S(2)}) collective-permute-start(bf16[128,1536]{1,0:T(8,128)(2,1)} %get-tuple-element.161), channel_id=1, source_target_pairs={{0,1},{1,2},{2,3},{3,0},{4,5},{5,6},{6,7},{7,4},{8,9},{9,10},{10,1... | collective-permute-start | bytes 1179656 | tf_op jit(solution)/shard_map/ppermute | solution.py:941
  206.6 21.3 %collective-permute-start.35 = (bf16[128,1536]{1,0:T(8,128)(2,1)}, bf16[128,1536]{1,0:T(8,128)(2,1)S(1)}, u32[]{:S(2)}, u32[]{:S(2)}) collective-permute-start(bf16[128,1536]{1,0:T(8,128)(2,1)} %get-tuple-element.162), channel_id=1, source_target_pairs={{0,3},{1,0},{2,1},{3,2},{4,7},{5,4},{6,5},{7,6},{8,11},{9,8},{10,9... | collective-permute-start | bytes 1179656 | tf_op jit(solution)/shard_map/ppermute | solution.py:941
  209.8 18.1 %collective-permute-start.36 = (bf16[128,1536]{1,0:T(8,128)(2,1)}, bf16[128,1536]{1,0:T(8,128)(2,1)S(1)}, u32[]{:S(2)}, u32[]{:S(2)}) collective-permute-start(bf16[128,1536]{1,0:T(8,128)(2,1)} %get-tuple-element.163), channel_id=1, source_target_pairs={{0,2},{1,3},{2,0},{3,1},{4,6},{5,7},{6,4},{7,5},{8,10},{9,11},{10,... | collective-permute-start | bytes 1179656 | tf_op jit(solution)/shard_map/ppermute | solution.py:941
  232.2 105.7 %reduce-scatter.8.cloned.1.call-start = ((), (), s32[]{:S(2)}) async-start(), calls=%async_computation.5 | async-start | bytes 1966080 | tf_op jit(solution)/shard_map/reduce_scatter | solution.py:1101
  233.2 13.5 %collective-permute-start.37 = (bf16[128,1664]{1,0:T(8,128)(2,1)S(1)}, bf16[128,1664]{1,0:T(8,128)(2,1)S(1)}, u32[]{:S(2)}, u32[]{:S(2)}) collective-permute-start(bf16[128,1664]{1,0:T(8,128)(2,1)S(1)} %copy-done.16), channel_id=1, source_target_pairs={{0,1},{1,2},{2,3},{3,0},{4,5},{5,6},{6,7},{7,4},{8,9},{9,10},{10,1... | collective-permute-start | bytes 1277960 | tf_op jit(solution)/shard_map/ppermute | solution.py:941
  233.8 20.4 %collective-permute-start.38 = (bf16[128,1664]{1,0:T(8,128)(2,1)S(1)}, bf16[128,1664]{1,0:T(8,128)(2,1)S(1)}, u32[]{:S(2)}, u32[]{:S(2)}) collective-permute-start(bf16[128,1664]{1,0:T(8,128)(2,1)S(1)} %copy-done.16), channel_id=1, source_target_pairs={{0,3},{1,0},{2,1},{3,2},{4,7},{5,4},{6,5},{7,6},{8,11},{9,8},{10,9... | collective-permute-start | bytes 1277960 | tf_op jit(solution)/shard_map/ppermute | solution.py:941
  236.4 19.2 %collective-permute-start.39 = (bf16[128,1664]{1,0:T(8,128)(2,1)S(1)}, bf16[128,1664]{1,0:T(8,128)(2,1)S(1)}, u32[]{:S(2)}, u32[]{:S(2)}) collective-permute-start(bf16[128,1664]{1,0:T(8,128)(2,1)S(1)} %copy-done.16), channel_id=1, source_target_pairs={{0,2},{1,3},{2,0},{3,1},{4,6},{5,7},{6,4},{7,5},{8,10},{9,11},{10,... | collective-permute-start | bytes 1277960 | tf_op jit(solution)/shard_map/ppermute | solution.py:941
  299.9 13.2 %collective-permute-start.41 = (bf16[192,1536]{1,0:T(8,128)(2,1)S(1)}, bf16[192,1536]{1,0:T(8,128)(2,1)S(1)}, u32[]{:S(2)}, u32[]{:S(2)}) collective-permute-start(bf16[192,1536]{1,0:T(8,128)(2,1)S(1)} %get-tuple-element.193), channel_id=1, source_target_pairs={{0,16},{4,20},{8,24},{12,28},{16,32},{20,36},{24,40},{28,44},{32,4... | collective-permute-start | bytes 1769480 | tf_op jit(solution)/shard_map/ppermute | solution.py:964
  301.3 9.7 %collective-permute-start.42 = (bf16[192,1152]{1,0:T(8,128)(2,1)S(1)}, bf16[192,1152]{1,0:T(8,128)(2,1)S(1)}, u32[]{:S(2)}, u32[]{:S(2)}) collective-permute-start(bf16[192,1152]{1,0:T(8,128)(2,1)S(1)} %get-tuple-element.194), channel_id=1, source_target_pairs={{0,48},{4,52},{8,56},{12,60},{16,0},{20,4},{24,8},{28,12},{32,16},... | collective-permute-start | bytes 1327112 | tf_op jit(solution)/shard_map/ppermute | solution.py:964
  313.4 15.9 %collective-permute-start.43 = (bf16[192,2688]{1,0:T(8,128)(2,1)S(1)}, bf16[192,2688]{1,0:T(8,128)(2,1)S(1)}, u32[]{:S(2)}, u32[]{:S(2)}) collective-permute-start(bf16[192,2688]{1,0:T(8,128)(2,1)S(1)} %get-tuple-element.199), channel_id=1, source_target_pairs={{0,16},{4,20},{8,24},{12,28},{16,32},{20,36},{24,40},{28,44},{32,4... | collective-permute-start | bytes 3096584 | tf_op jit(solution)/shard_map/ppermute | solution.py:964
  313.5 15.8 %collective-permute-start.44 = (bf16[192,2688]{1,0:T(8,128)(2,1)S(1)}, bf16[192,2688]{1,0:T(8,128)(2,1)S(1)}, u32[]{:S(2)}, u32[]{:S(2)}) collective-permute-start(bf16[192,2688]{1,0:T(8,128)(2,1)S(1)} %get-tuple-element.200), channel_id=1, source_target_pairs={{0,48},{4,52},{8,56},{12,60},{16,0},{20,4},{24,8},{28,12},{32,16},... | collective-permute-start | bytes 3096584 | tf_op jit(solution)/shard_map/ppermute | solution.py:964
  349.7 9.8 %collective-permute-start.47 = (f32[128,1536]{1,0:T(8,128)}, f32[128,1536]{1,0:T(8,128)}, u32[]{:S(2)}, u32[]{:S(2)}) collective-permute-start(f32[128,1536]{1,0:T(8,128)} %broadcast_select_fusion), channel_id=1, source_target_pairs={{0,64},{64,0},{1,65},{65,1},{2,66},{66,2},{3,67},{67,3},{4,68},{68... | collective-permute-start | bytes 2359304 | tf_op jit(solution)/shard_map/ppermute | solution.py:937
  352.7 9.6 %collective-permute-start.51 = (f32[32,256]{1,0:T(8,128)S(1)}, f32[32,256]{1,0:T(8,128)S(1)}, u32[]{:S(2)}, u32[]{:S(2)}) collective-permute-start(f32[32,256]{1,0:T(8,128)S(1)} %get-tuple-element.260), channel_id=1, source_target_pairs={{0,1},{1,2},{2,3},{3,0},{4,5},{5,6},{6,7},{7,4},{8,9},{9,10},{10,1... | collective-permute-start | bytes 98312 | tf_op jit(solution)/shard_map/ppermute | solution.py:941
  353.0 9.2 %collective-permute-start.52 = (f32[32,256]{1,0:T(8,128)S(1)}, f32[32,256]{1,0:T(8,128)S(1)}, u32[]{:S(2)}, u32[]{:S(2)}) collective-permute-start(f32[32,256]{1,0:T(8,128)S(1)} %get-tuple-element.259), channel_id=1, source_target_pairs={{0,3},{1,0},{2,1},{3,2},{4,7},{5,4},{6,5},{7,6},{8,11},{9,8},{10,9... | collective-permute-start | bytes 98312 | tf_op jit(solution)/shard_map/ppermute | solution.py:941
  (69 other events, 517.4 us)
Sparse Core Ops, SparseCore 0:
  21.9 40.5 all-gather.5
  71.9 48.9 all-gather.3
  167.5 24.3 reduce-scatter.5
  232.3 77.9 reduce-scatter.9
  313.5 24.3 reduce-scatter.7
where the time goes:
time: 380 us; the launch traced here: 373 us
  waiting for transfers between devices  138 us (36%)
  Pallas kernels  117 us (31%)
  starting transfers between devices  62.7 us (16%)
  local copies, waits for them, and re-layouts  32 us (8%)
  between operations  15 us (4%)
  other arithmetic  7.96 us (2%)
    pallas_call x2, Pallas kernels, backward_call(): pl.pallas_call(kernel, out_shape=out_shape, in_specs=in_specs, out_specs=...  60.6 us
    ppermute x19, waiting for transfers between devices, ring(): return lax.ppermute(v, ('section', *DP), pairs)  59.6 us
    ppermute x21, waiting for transfers between devices, turn(): return lax.ppermute(v, axis, [(i, (i + by) % 4) for i in range(4)])  59.4 us
    pallas_call x2, Pallas kernels, forward_call(): pl.pallas_call(kernel, out_shape=out_shape, in_specs=in_specs, out_specs=...  37.2 us
    ppermute x21, starting transfers between devices, turn(): return lax.ppermute(v, axis, [(i, (i + by) % 4) for i in range(4)])  30.4 us
    ppermute x19, starting transfers between devices, ring(): return lax.ppermute(v, ('section', *DP), pairs)  27.9 us
    unnamed x102, local copies, waits for them, and re-layouts  19.1 us
    ppermute x14, waiting for transfers between devices, swap(): return lax.ppermute(v, 'section', [(0, 1), (1, 0)])  16.6 us
  transfers between devices with their start and end apart: 59, of which 32 were waited for; matrix products, arithmetic and copies ran while one was open for 5% of the time, Pallas kernels for 25%

commit v1 on v0

--- a/solution.py
+++ b/solution.py
@@ -31,15 +31,20 @@
 ANY = pl.BlockSpec(memory_space=pl.ANY)
 SIDE = D // 2
 WIDE = 2 * CHANNELS + CHANNELS + 384
-IN = slice(0, 2 * CHANNELS)
-OUT = slice(2 * CHANNELS, 3 * CHANNELS)
-SS = slice(3 * CHANNELS, WIDE)
-STATE = slice(3 * CHANNELS, 3 * CHANNELS + 256)
-MISC = slice(3 * CHANNELS + 256, WIDE)
+SS = slice(0, 384)
+STATE = slice(0, 256)
+MISC = slice(256, 384)
+Z = slice(384, 384 + CHANNELS)
+X = slice(384 + CHANNELS, 384 + 2 * CHANNELS)
+IN = slice(384, 384 + 2 * CHANNELS)
+READ = 384 + 2 * CHANNELS
+BOTH = slice(0, READ)
+OUT = slice(READ, WIDE)
 MAIN = 3 * CHANNELS
 SPLIT = 2 * CHANNELS
 PART = 256
 LEFT, RIGHT = slice(0, SPLIT), slice(SPLIT, WIDE)
+BETWEEN = slice(SPLIT, READ)
 VMEM_LIMIT = 54
 
 
@@ -248,29 +253,29 @@
         taps_ref, taps_state_ref, heads_ref, gain_ref = take(4)
     else:
         own_in, other_in, (heads_ref,) = take(5), take(5), take(1)
-    normed_out, zx_out, ss_out, y_out, starts_out, gg_out = take(6)
+    normed_out, read_out, y_out, starts_out, gg_out = take(5)
     if last:
         dscaled_out, stats, mixed_out = take(3)
     else:
         outs = take(4)
         taps_ref, taps_state_ref, gain_ref = take(3)
-    normed, zx, ss, y_all, starts, gated_gain, whole = take(7)
+    normed, read, y_all, starts, gated_gain, whole = take(6)
     x_pad, state_pad, x_conv, state_conv, hidden, sems, held_rows = take(7)
     if last:
         dscaled, mixed = take(2)
     copies = Copies(sems)
     place, core = where_ref[0], where_ref[1]
     weights = (own_in, other_in)
-    if not last:
+    if last:
+        load_in = place_blocks(copies, where_ref, weights, whole, BOTH)
+        load_rest = place_blocks(copies, where_ref, weights, whole, OUT)
+    else:
         load_rows = [
             copies.start(ends.at[k, 0], held_rows.at[rows_at(k), :]) for k in range(BLOCKS)
         ]
-        load_rest = place_blocks(copies, where_ref, weights, whole, RIGHT)
-    load_in = place_blocks(copies, where_ref, weights, whole, LEFT)
-    if last:
-        load_rest = place_blocks(copies, where_ref, weights, whole, RIGHT)
-    else:
-        for load in load_rest + load_rows:
+        load_first = place_blocks(copies, where_ref, weights, whole, LEFT)
+        load_in = place_blocks(copies, where_ref, weights, whole, RIGHT)
+        for load in load_rows + load_first:
             load.wait()
         small_params(place, whole.at[:, MISC], heads_ref, taps_ref, taps_state_ref, gain_ref)
     for k, offset in enumerate((0, 3, 1, 2)):
@@ -285,20 +290,17 @@
         ]
     for load in load_in:
         load.wait()
-    zx[...] = dot_nn(normed[...], whole[:, IN])
-    copies.store(zx, zx_out)
+    read[...] = dot_nn(normed[...], whole[:, BOTH])
+    copies.store(read, read_out)
     if last:
         for load in load_rest + load_rows:
             load.wait()
-    ss[...] = dot_nn(normed[...], whole[:, SS])
-    copies.store(ss, ss_out)
-    if last:
         dscaled[...] = dot_nn(held_rows[...], whole[:, OUT])
         copies.store(dscaled, dscaled_out)
     x_pad[:PAD, :] = jnp.zeros((PAD, CHANNELS), F32)
-    x_pad[PAD:, :] = zx[:, CHANNELS:]
+    x_pad[PAD:, :] = read[:, X]
     state_pad[:PAD, :] = jnp.zeros((PAD, 2 * STATES), F32)
-    state_pad[PAD:, :] = ss[:, : 2 * STATES]
+    state_pad[PAD:, :] = read[:, STATE]
     hidden[...] = jnp.zeros_like(hidden)
     conv_rows(x_pad, taps_ref, x_conv)
     conv_rows(state_pad, taps_state_ref, state_conv)
@@ -309,7 +311,7 @@
         state = state_u * sigmoid(state_u)
         keys, reads = state[:, :STATES].astype(BF), state[:, STATES:].astype(BF)
         keys_t = jnp.transpose(state[:, :STATES]).astype(BF)
-        _, step, _, summed, summed_t = step_terms(ss[rows, 2 * STATES :], heads_ref)
+        _, step, _, summed, summed_t = step_terms(read[rows, MISC], heads_ref)
         meets = dot_nt(reads, keys)
         causal = iota((BLOCK, BLOCK), 0) >= iota((BLOCK, BLOCK), 1)
         squares = jnp.zeros((BLOCK, 128), F32)
@@ -337,7 +339,7 @@
                 keys_t, (to_end * weighted).astype(BF)
             )
             y_all[rows, cols] = y
-            z = zx[rows, cols]
+            z = read[rows, Z.start + p * 128 : Z.start + (p + 1) * 128]
             gated = y * z * sigmoid(z)
             squares = squares + gated * gated
             gained = gated * taps_ref[5:6, cols]
@@ -388,13 +390,12 @@
     last = len(chunks) > 0
     kept = [
         shape(SEQ, D, dtype=BF),
-        shape(SEQ, 2 * CHANNELS),
-        shape(SEQ, 384),
+        shape(SEQ, READ),
         shape(SEQ, CHANNELS),
         shape(BLOCKS, STATES, CHANNELS, dtype=BF),
         shape(SEQ, CHANNELS, dtype=BF),
     ]
-    out_shape, out_specs = in_hbm(kept), [HBM] * 6
+    out_shape, out_specs = in_hbm(kept), [HBM] * 5
     scratch = [pltpu.VMEM(k.shape, k.dtype) for k in kept] + [pltpu.VMEM((D, WIDE), BF)]
     scratch += [
         pltpu.VMEM((PAD + SEQ, CHANNELS), F32),
@@ -471,7 +472,7 @@
         return taken
 
     (where_ref,) = take(1)
-    normed_in, zx_in, ss_in, y_in, starts_in, gated_gain_in = take(6)
+    normed_in, read_in, y_in, starts_in, gated_gain_in = take(5)
     weights = (take(1), take(1)) if last else (take(5), take(5))
     taps_ref, taps_state_ref, heads_ref, gain_ref = take(4)
     if last:
@@ -482,18 +483,18 @@
     outs = take(4 if last else 1)
     (grad_small,) = take(1)
     mine_out, theirs_out = take(2)
-    normed, zx, ss, y_all, starts, gated_gain, whole, dscaled = take(8)
+    normed, read, y_all, starts, gated_gain, whole, dscaled = take(7)
     x_pad, state_pad, x_conv, state_conv, du_pad, dstate_pad = take(6)
-    d_hidden, d_inner, factors, sems = take(4)
-    dss, products, rows_grad, sent = take(4)
+    d_hidden, d_read, factors, sems = take(4)
+    products, rows_grad, sent = take(3)
     grad_taps, grad_taps_state = grad_small.at[0:8, 0:CHANNELS], grad_small.at[0:8, 768:1024]
     grad_heads, grad_gain = grad_small.at[0:8, 1024:1152], grad_small.at[8:9, :]
     copies = Copies(sems)
     place, core = where_ref[0], where_ref[1]
     if not last:
         load_out = place_blocks(copies, where_ref, weights, whole, OUT)
-    load_x = copies.start(zx_in.at[:, CHANNELS:], zx.at[:, CHANNELS:])
-    load_ss = copies.start(ss_in, ss)
+    load_x = copies.start(read_in.at[:, X], read.at[:, X])
+    load_ss = copies.start(read_in.at[:, SS], read.at[:, SS])
     if last:
         load_cot = [copies.start(cot.at[k, 1], sent.at[rows_at(k), :]) for k in range(BLOCKS)]
     du_pad[SEQ:, :] = jnp.zeros((PAD, CHANNELS), F32)
@@ -529,17 +530,17 @@
         rows_grad[...] = scaled_rows(rows_grad[...], factors[:, 0:1])
     load_x.wait()
     load_rows = [
-        copies.start(zx_in.at[:, :CHANNELS], zx.at[:, :CHANNELS]),
+        copies.start(read_in.at[:, Z], read.at[:, Z]),
         copies.start(y_in, y_all),
         copies.start(starts_in, starts),
     ]
     if last:
         load_rows.append(copies.start(dscaled_in, dscaled))
     x_pad[:PAD, :] = jnp.zeros((PAD, CHANNELS), F32)
-    x_pad[PAD:, :] = zx[:, CHANNELS:]
+    x_pad[PAD:, :] = read[:, X]
     load_ss.wait()
     state_pad[:PAD, :] = jnp.zeros((PAD, 2 * STATES), F32)
-    state_pad[PAD:, :] = ss[:, : 2 * STATES]
+    state_pad[PAD:, :] = read[:, STATE]
     conv_rows(x_pad, taps_ref, x_conv)
     conv_rows(state_pad, taps_state_ref, state_conv)
     for load in load_rows:
@@ -547,9 +548,9 @@
     load_late = [
         copies.start(normed_in, normed),
         copies.start(gated_gain_in, gated_gain),
-        *place_blocks(copies, where_ref, weights, whole, IN),
-        *place_blocks(copies, where_ref, weights, whole, SS),
     ]
+    for cols in (BOTH,) if last else (LEFT, BETWEEN):
+        load_late += place_blocks(copies, where_ref, weights, whole, cols)
 
     def block(turn, carry):
         b = BLOCKS - 1 - turn
@@ -559,7 +560,7 @@
         state = state_u * state_s
         keys, reads = state[:, :STATES].astype(BF), state[:, STATES:].astype(BF)
         reads_t = jnp.transpose(state[:, STATES:]).astype(BF)
-        raised, step, log_decay, summed, summed_t = step_terms(ss[rows, 2 * STATES :], heads_ref)
+        raised, step, log_decay, summed, summed_t = step_terms(read[rows, MISC], heads_ref)
         meets_t = dot_nt(keys, reads)
         causal_t = iota((BLOCK, BLOCK), 1) >= iota((BLOCK, BLOCK), 0)
         fac = factors[rows, :][:, 0:1]
@@ -581,7 +582,7 @@
             to_end = jnp.exp(summed_wide[BLOCK - 1 : BLOCK, :] - summed_wide)
             skip = taps_ref[6:7, cols]
             gain = taps_ref[5:6, cols]
-            z = zx[rows, cols]
+            z = read[rows, Z.start + p * 128 : Z.start + (p + 1) * 128]
             zs = sigmoid(z)
             z_act = z * zs
             y = y_all[rows, cols]
@@ -591,7 +592,7 @@
             grad_taps[5:6, cols] += jnp.sum(incoming * lifted, axis=0, keepdims=True)
             d_gated = fac * (gain * incoming) - gated * cub
             dy = d_gated * z_act
-            d_inner[rows, cols] = (d_gated * y * (zs + z_act * (1.0 - zs))).astype(BF)
+            d_read[rows, Z.start + p * 128 : Z.start + (p + 1) * 128] = (d_gated * y * (zs + z_act * (1.0 - zs))).astype(BF)
             dy_low = dy.astype(BF)
             weighted = x * step_wide
             weighted_low = weighted.astype(BF)
@@ -634,7 +635,7 @@
         d_decay = dot_high(upper_tri, head_sums[:BLOCK])
         d_step = head_sums[BLOCK:] - d_decay * jnp.exp(heads_ref[1:2, :])
         d_raw = d_step * sigmoid(raised)
-        dss[rows, 2 * STATES :] = d_raw.astype(BF)
+        d_read[rows, MISC] = d_raw.astype(BF)
         grad_heads[0:1, :] += jnp.sum(d_raw, axis=0, keepdims=True)
         grad_heads[1:2, :] += jnp.sum(d_decay * log_decay, axis=0, keepdims=True)
         return carry
@@ -642,11 +643,11 @@
     lax.fori_loop(0, BLOCKS, block, 0)
 
     def store_inner(start, cols, value):
-        cols = slice(CHANNELS + cols.start, CHANNELS + cols.stop)
-        d_inner[start : start + BLOCK, cols] = value
+        cols = slice(X.start + cols.start, X.start + cols.stop)
+        d_read[start : start + BLOCK, cols] = value
 
     def store_state(start, cols, value):
-        dss[start : start + BLOCK, cols] = value
+        d_read[start : start + BLOCK, cols] = value
 
     conv_back(du_pad, x_pad, taps_ref, grad_taps, store_inner)
     conv_back(dstate_pad, state_pad, taps_state_ref, grad_taps_state, store_state)
@@ -656,7 +657,7 @@
         load.wait()
     for at in range(0, D, PART):
         cols = slice(at, at + PART)
-        part = dot_nt(d_inner[...], whole[cols, IN]) + dot_nt(dss[...], whole[cols, SS])
+        part = dot_nt(d_read[...], whole[cols, BOTH])
         total = jnp.sum(part * normed[:, cols].astype(F32), axis=0, keepdims=True)
         grad_gain[:, cols] = total / gain_ref[:, cols]
         sent[:, cols] = part.astype(BF)
@@ -668,12 +669,12 @@
     parts = misc_parts(grad_small)
     for i in range(4):
         lanes = slice(i * 384, (i + 1) * 384)
-        shared = dot_tn(normed[:, lanes], dss[...])
+        shared = dot_tn(normed[:, lanes], d_read[...])
         for cols, value in (
-            (IN, dot_tn(normed[:, lanes], d_inner[...])),
+            (STATE, shared[:, STATE]),
+            (MISC, shared[:, MISC] + misc_tile(i, place, parts, grad_small)),
+            (IN, shared[:, IN]),
             (OUT, dot_tn(rows_grad[:, lanes], gated_gain[...])),
-            (STATE, shared[:, :256]),
-            (MISC, shared[:, 256:] + misc_tile(i, place, parts, grad_small)),
         ):
             low = value.astype(BF)
             for k in range(8):
@@ -687,7 +688,7 @@
 
 def backward_call(where, kept, weights, taps, taps_state, heads, gain, last, extra):
     args = [where, *kept, *weights, taps, taps_state, heads, gain, *extra]
-    in_specs = [SMEM] + [HBM] * 6 + [ANY] * len(weights) + [VMEM] * 4
+    in_specs = [SMEM] + [HBM] * 5 + [ANY] * len(weights) + [VMEM] * 4
     in_specs += [HBM, ANY] + [VMEM] * 4 if last else [VMEM] * 4
     out_shape = [
         *([pltpu.HBM((BLOCK, D), BF)] * 4 if last else [pltpu.HBM((SEQ, D), BF)]),
@@ -705,10 +706,9 @@
         pltpu.VMEM((PAD + SEQ, CHANNELS), F32),
         pltpu.VMEM((PAD + SEQ, 2 * STATES), F32),
         pltpu.VMEM((STATES, CHANNELS), F32),
-        pltpu.VMEM((SEQ, 2 * CHANNELS), BF),
+        pltpu.VMEM((SEQ, READ), BF),
         pltpu.VMEM((SEQ, 128), F32),
         pltpu.SemaphoreType.DMA((128,)),
-        pltpu.VMEM((SEQ, 384), BF),
         pltpu.VMEM((2, SIDE, WIDE), BF),
         pltpu.VMEM((SEQ, D), BF),
         pltpu.VMEM((SEQ, D), BF),
@@ -980,7 +980,7 @@
     far = jnp.concatenate([far_left, far_right], axis=1)
     rest = (rest, ring(rest, -1, 0), ring(rest, 2, 0), ring(rest, 1, 0))
     rows = [
-        jnp.concatenate(pair, axis=1) for pair in zip((own, ahead, far, behind), rest)
+        jnp.concatenate(pair, axis=1) for pair in zip(rest, (own, ahead, far, behind))
     ]
     return around(jnp.concatenate(rows, axis=0), 1)
 
@@ -1012,13 +1012,26 @@
         [place, core, lax.axis_index("dp_0"), lax.axis_index("dp_1")]
     ).astype(jnp.int32)
 
+    def by_layer_of(keep, got):
+        return jnp.where(is_first, keep, got), jnp.where(is_first, got, keep)
+
+    def by_layer(halves):
+        return by_layer_of(pick(halves, core, 0), swap(pick(halves, 1 - core, 0)))
+
+    main = jnp.concatenate([proj_inner[0].reshape(96, 2 * CHANNELS), proj_output[0].T], axis=1)
+    main_0, main_1 = by_layer(main.reshape(2, 48, MAIN))
+    main_0, heads_got, *small = tie(
+        main_0,
+        swap(head_params[0]),
+        proj_state[0],
+        norm_gain[0],
+        conv_inner[0],
+        gate_gain[0],
+        conv_state[0],
+    )
     packed = jnp.concatenate(
         [
-            proj_state[0].reshape(-1),
-            norm_gain[0],
-            conv_inner[0].reshape(-1),
-            gate_gain[0],
-            conv_state[0].reshape(-1),
+            *[v.reshape(-1) for v in small],
             jnp.zeros((32 * 256 - 6144 - 332,), BF),
         ]
     ).reshape(32, 256)
@@ -1036,15 +1049,6 @@
         [proj_step[0], both, norm_col, state_cols, jnp.zeros((96, 128 - 30), BF)], axis=1
     )
 
-    def by_layer_of(keep, got):
-        return jnp.where(is_first, keep, got), jnp.where(is_first, got, keep)
-
-    def by_layer(halves):
-        return by_layer_of(pick(halves, core, 0), swap(pick(halves, 1 - core, 0)))
-
-    main = jnp.concatenate([proj_inner[0].reshape(96, 2 * CHANNELS), proj_output[0].T], axis=1)
-    main_0, main_1 = by_layer(main.reshape(2, 48, MAIN))
-    main_0, heads_got = tie(main_0, swap(head_params[0]))
     rest_0, rest_1 = by_layer(jnp.concatenate([state_rows, misc], axis=1).reshape(2, 48, 384))
 
     ends = section_ends[0]
@@ -1057,13 +1061,13 @@
     ]
     ends_all = lax.all_gather(jnp.stack([rows_in, cot]), "tensor", axis=0)
     own_pieces = gather_by_turns(main_0, rest_0)
-    shard_1 = jnp.concatenate([main_1, rest_1], axis=1)
+    shard_1 = jnp.concatenate([rest_1, main_1], axis=1)
     shard_1, *rest = tie(shard_1, *heads, *own_pieces)
     heads, own_pieces = rest[:2], rest[2:]
     full_1 = lax.all_gather(shard_1, DP, axis=0, tiled=True)
     pieces_0 = (*own_pieces, *[swap(v) for v in own_pieces])
     first = forward_call(where, ends_all, (), (*pieces_0, heads[0]))
-    kept_0, sent_0, small_0 = first[:6], first[6:10], first[10:]
+    kept_0, sent_0, small_0 = first[:5], first[5:9], first[9:]
     weights_0 = (pieces_0, small_0[0], small_0[1], heads[0], small_0[2])
     own_1, *met_0 = tie(full_1, *meet(sent_0))
     other_1 = swap(own_1)
@@ -1075,11 +1079,11 @@
     kept_1 = forward_call(
         where, ends_all, spread_rows(hidden), (own_1, other_1, *weights_1[1:])
     )
-    dscaled_1, stats, mixed_1 = kept_1[6:]
+    dscaled_1, stats, mixed_1 = kept_1[5:]
     stat_parts = spread_rows(stats)
     met_1 = lax.psum_scatter(mixed_1, "tensor", scatter_dimension=0, tiled=True)
     back_1 = backward_call(
-        where, kept_1[:6], *weights_1, True, (dscaled_1, ends_all, *stat_parts)
+        where, kept_1[:5], *weights_1, True, (dscaled_1, ends_all, *stat_parts)
     )
     met_1, *back_1 = tie(met_1, *back_1)
     payload_1 = both_call(where, back_1[5], swap(back_1[6]), False)[0]

time: 380 us -> 376 us (0.989)
    unnamed x102 -> x113, local copies, waits for them, and re-layouts: 19.1 us -> 17.7 us
  transfers between devices with their start and end apart: 59 -> 59, of which waited for: 32 -> 35; matrix products, arithmetic and copies ran while one was open for 5% -> 5% of each run, Pallas kernels for 25% -> 25%
where the time goes in v1:
time: 376 us; the launch traced here: 368 us
  waiting for transfers between devices  138 us (37%)
  Pallas kernels  117 us (31%)
  starting transfers between devices  62 us (16%)
  local copies, waits for them, and re-layouts  28.7 us (8%)
  between operations  15.1 us (4%)
  other arithmetic  7.91 us (2%)
    ppermute x21, waiting for transfers between devices, turn(): return lax.ppermute(v, axis, [(i, (i + by) % 4) for i in range(4)])  60.8 us
    pallas_call x2, Pallas kernels, backward_call(): pl.pallas_call(kernel, out_shape=out_shape, in_specs=in_specs, out_specs=...  60.5 us
    ppermute x19, waiting for transfers between devices, ring(): return lax.ppermute(v, ('section', *DP), pairs)  58.7 us
    pallas_call x2, Pallas kernels, forward_call(): pl.pallas_call(kernel, out_shape=out_shape, in_specs=in_specs, out_specs=...  36.9 us
    ppermute x21, starting transfers between devices, turn(): return lax.ppermute(v, axis, [(i, (i + by) % 4) for i in range(4)])  29.7 us
    ppermute x19, starting transfers between devices, ring(): return lax.ppermute(v, ('section', *DP), pairs)  27.8 us
    unnamed x113, local copies, waits for them, and re-layouts  17.7 us
    ppermute x14, waiting for transfers between devices, swap(): return lax.ppermute(v, 'section', [(0, 1), (1, 0)])  16.6 us
  transfers between devices with their start and end apart: 59, of which 35 were waited for; matrix products, arithmetic and copies ran while one was open for 5% of the time, Pallas kernels for 25%

profile of v1, /device:TPU:0, one launch (start us, length us, event | category | flops | bytes accessed | tf_op | source)
XLA Modules:
  0.0 368.3 jit_solution(13424069668121401793)
XLA Ops:
  13.1 4.2 %collective-permute-start.3 = (bf16[32,256]{1,0:T(8,128)(2,1)S(1)}, bf16[32,256]{1,0:T(8,128)(2,1)S(1)}, u32[]{:S(2)}, u32[]{:S(2)}) collective-permute-start(bf16[32,256]{1,0:T(8,128)(2,1)S(1)} %reshape.109), channel_id=1, source_target_pairs={{0,3},{1,0},{2,1},{3,2},{4,7},{5,4},{6,5},{7,6},{8,11},{9,8},{10,9... | collective-permute-start | bytes 49160 | tf_op jit(solution)/shard_map/ppermute | solution.py:941
  18.5 3.0 collective-permute-start.8
  25.0 3.7 %collective-permute-done.9 = bf16[48,2304]{1,0:T(8,128)(2,1)S(1)} collective-permute-done((bf16[48,2304]{1,0:T(8,128)(2,1)S(1)}, bf16[48,2304]{1,0:T(8,128)(2,1)S(1)}, u32[]{:S(2)}, u32[]{:S(2)}) %collective-permute-start.9) | collective-permute-done | bytes 221216 | tf_op jit(solution)/shard_map/ppermute | solution.py:964
  28.7 3.3 collective-permute-start.11
  39.3 3.0 collective-permute-start.14
  42.3 12.1 %collective-permute-done.14.refs_3_.refs_7_ = bf16[192,2688]{1,0:T(8,128)(2,1)S(1)} collective-permute-done((bf16[192,2688]{1,0:T(8,128)(2,1)S(1)}, bf16[192,2688]{1,0:T(8,128)(2,1)S(1)}, u32[]{:S(2)}, u32[]{:S(2)}) %collective-permute-start.14) | collective-permute-done | bytes 1032224 | tf_op jit(solution)/shard_map/ppermute | solution.py:964
  54.4 3.7 %collective-permute-done.15.refs_6_.refs_10_ = bf16[192,2688]{1,0:T(8,128)(2,1)S(1)} collective-permute-done((bf16[192,2688]{1,0:T(8,128)(2,1)S(1)}, bf16[192,2688]{1,0:T(8,128)(2,1)S(1)}, u32[]{:S(2)}, u32[]{:S(2)}) %collective-permute-start.15) | collective-permute-done | bytes 1032224 | tf_op jit(solution)/shard_map/ppermute | solution.py:964
  61.7 6.3 %collective-permute-done.17.refs_5_.refs_9_ = bf16[192,1152]{1,0:T(8,128)(2,1)} collective-permute-done((bf16[192,1152]{1,0:T(8,128)(2,1)S(1)}, bf16[192,1152]{1,0:T(8,128)(2,1)}, u32[]{:S(2)}, u32[]{:S(2)}) %collective-permute-start.17) | collective-permute-done | bytes 442400 | tf_op jit(solution)/shard_map/ppermute | solution.py:964
  70.2 5.4 %collective-permute-done.21.refs_10_.refs_14_ = bf16[192,1152]{1,0:T(8,128)(2,1)S(1)} collective-permute-done((bf16[192,1152]{1,0:T(8,128)(2,1)}, bf16[192,1152]{1,0:T(8,128)(2,1)S(1)}, u32[]{:S(2)}, u32[]{:S(2)}) %collective-permute-start.21) | collective-permute-done | bytes 442400 | tf_op jit(solution)/shard_map/ppermute | solution.py:937
  76.6 17.3 %layer_forward.2 = (bf16[512,1536]{1,0:T(8,128)(2,1)}, f32[512,1920]{1,0:T(8,128)}, f32[512,768]{1,0:T(8,128)}, bf16[4,128,768]{2,1,0:T(8,128)(2,1)}, bf16[512,7...) custom-call(s32[4]{0:T(128)} %pad_add_fusion.refs_0_.where_ref, ...), custom_call_target="tpu_custom_call" | custom-call | flops 20000000000 | bytes 24000000 | tf_op jit(solution)/shard_map/layer_forward/pallas_call | solution.py:425
  98.2 9.6 %collective-permute-done.23.b = bf16[128,1664]{1,0:T(8,128)(2,1)S(1)} collective-permute-done((bf16[128,1664]{1,0:T(8,128)(2,1)}, bf16[128,1664]{1,0:T(8,128)(2,1)S(1)}, u32[]{:S(2)}, u32[]{:S(2)}) %collective-permute-start.23) | collective-permute-done | bytes 426016 | tf_op jit(solution)/shard_map/ppermute | solution.py:941
  109.0 7.5 %collective-permute-done.25.d = bf16[128,1664]{1,0:T(8,128)(2,1)S(1)} collective-permute-done((bf16[128,1664]{1,0:T(8,128)(2,1)}, bf16[128,1664]{1,0:T(8,128)(2,1)S(1)}, u32[]{:S(2)}, u32[]{:S(2)}) %collective-permute-start.25) | collective-permute-done | bytes 426016 | tf_op jit(solution)/shard_map/ppermute | solution.py:941
  117.3 2.9 between_layers.1
  133.7 8.8 %collective-permute-done.28.refs_5_ = bf16[128,1536]{1,0:T(8,128)(2,1)S(1)} collective-permute-done((bf16[128,1536]{1,0:T(8,128)(2,1)}, bf16[128,1536]{1,0:T(8,128)(2,1)S(1)}, u32[]{:S(2)}, u32[]{:S(2)}) %collective-permute-start.28) | collective-permute-done | bytes 393248 | tf_op jit(solution)/shard_map/ppermute | solution.py:941
  143.3 19.7 %layer_forward.3 = (bf16[512,1536]{1,0:T(8,128)(2,1)}, f32[512,1920]{1,0:T(8,128)}, f32[512,768]{1,0:T(8,128)}, bf16[4,128,768]{2,1,0:T(8,128)(2,1)}, bf16[512,7...) custom-call(s32[4]{0:T(128)} %pad_add_fusion.refs_0_.where_ref, ...), custom_call_target="tpu_custom_call" | custom-call | flops 20000000000 | bytes 24000000 | tf_op jit(solution)/shard_map/layer_forward/pallas_call | solution.py:425
  168.2 3.5 collective-permute-done.32.refs_17_.d
  172.4 29.5 %layer_backward.2 = (bf16[128,1536]{1,0:T(8,128)(2,1)}, bf16[128,1536]{1,0:T(8,128)(2,1)}, bf16[128,1536]{1,0:T(8,128)(2,1)}, bf16[128,1536]{1,0:T(8,128)(2,1)},...) custom-call(s32[4]{0:T(128)} %pad_add_fusion.refs_0_.where_ref, ...), custom_call_target="tpu_custom_call" | custom-call | flops 32000000000 | bytes 30000000 | tf_op jit(solution)/shard_map/layer_backward/pallas_call | solution.py:720
  202.1 3.2 collective-permute-start.35
  205.5 3.8 %collective-permute-done.33.given = bf16[768,2688]{1,0:T(8,128)(2,1)S(1)} collective-permute-done((bf16[768,2688]{1,0:T(8,128)(2,1)}, bf16[768,2688]{1,0:T(8,128)(2,1)S(1)}, u32[]{:S(2)}, u32[]{:S(2)}) %collective-permute-start.33) | collective-permute-done | bytes 4128800 | tf_op jit(solution)/shard_map/ppermute | solution.py:937
  214.9 8.5 %collective-permute-done.34.b = bf16[128,1536]{1,0:T(8,128)(2,1)S(1)} collective-permute-done((bf16[128,1536]{1,0:T(8,128)(2,1)}, bf16[128,1536]{1,0:T(8,128)(2,1)S(1)}, u32[]{:S(2)}, u32[]{:S(2)}) %collective-permute-start.34) | collective-permute-done | bytes 393248 | tf_op jit(solution)/shard_map/ppermute | solution.py:941
  224.4 3.3 between_layers_back.1.refs_20_.grad_ref
  229.3 2.6 collective-permute-start.38
  235.4 6.9 %collective-permute-done.37.refs_21_ = bf16[128,1664]{1,0:T(8,128)(2,1)S(1)} collective-permute-done((bf16[128,1664]{1,0:T(8,128)(2,1)S(1)}, bf16[128,1664]{1,0:T(8,128)(2,1)S(1)}, u32[]{:S(2)}, u32[]{:S(2)}) %collective-permute-start.37) | collective-permute-done | bytes 426016 | tf_op jit(solution)/shard_map/ppermute | solution.py:941
  242.2 7.5 %collective-permute-done.38.refs_22_ = bf16[128,1664]{1,0:T(8,128)(2,1)S(1)} collective-permute-done((bf16[128,1664]{1,0:T(8,128)(2,1)S(1)}, bf16[128,1664]{1,0:T(8,128)(2,1)S(1)}, u32[]{:S(2)}, u32[]{:S(2)}) %collective-permute-start.38) | collective-permute-done | bytes 426016 | tf_op jit(solution)/shard_map/ppermute | solution.py:941
  251.9 31.0 %layer_backward.3 = (bf16[512,1536]{1,0:T(8,128)(2,1)}, f32[16,1536]{1,0:T(8,128)}, bf16[768,2688]{1,0:T(8,128)(2,1)}, bf16[768,2688]{1,0:T(8,128)(2,1)}) custom-call(s32[4]{0:T(128)} %pad_add_fusion.refs_0_.where_ref, bf16[512,1536]{1,0:T(8,128)(2,1)} %get-tuple-element.180.refs_1_, f32[512,1920]{1,0:T(8,128)} %get-tuple-element.181.refs_2_, ...), custom_call_target="tpu_custom_call" | custom-call | flops 32000000000 | bytes 30000000 | tf_op jit(solution)/shard_map/layer_backward/pallas_call | solution.py:720
  283.2 7.3 %collective-permute-done.40.given = bf16[768,2688]{1,0:T(8,128)(2,1)S(1)} collective-permute-done((bf16[768,2688]{1,0:T(8,128)(2,1)}, bf16[768,2688]{1,0:T(8,128)(2,1)S(1)}, u32[]{:S(2)}, u32[]{:S(2)}) %collective-permute-start.40) | collective-permute-done | bytes 4128800 | tf_op jit(solution)/shard_map/ppermute | solution.py:937
  298.7 7.9 %collective-permute-done.42.right = bf16[192,1152]{1,0:T(8,128)(2,1)S(1)} collective-permute-done((bf16[192,1152]{1,0:T(8,128)(2,1)S(1)}, bf16[192,1152]{1,0:T(8,128)(2,1)S(1)}, u32[]{:S(2)}, u32[]{:S(2)}) %collective-permute-start.42) | collective-permute-done | bytes 442400 | tf_op jit(solution)/shard_map/ppermute | solution.py:964
  309.1 3.2 collective-permute-start.44
  312.3 12.6 %collective-permute-done.43.b = bf16[192,2688]{1,0:T(8,128)(2,1)S(1)} collective-permute-done((bf16[192,2688]{1,0:T(8,128)(2,1)S(1)}, bf16[192,2688]{1,0:T(8,128)(2,1)S(1)}, u32[]{:S(2)}, u32[]{:S(2)}) %collective-permute-start.43) | collective-permute-done | bytes 1032224 | tf_op jit(solution)/shard_map/ppermute | solution.py:964
  326.7 2.6 collective-permute-start.46
  348.6 3.0 collective-permute-start.52
  355.2 2.7 maximum_select_fusion
  (299 shorter events, 103.7 us)
Async XLA Ops:
  7.2 68.6 %all-gather.6.cloned.1.call-start = ((), (), s32[]{:S(2)}) async-start(), calls=%async_computation.6 | async-start | bytes 3932160 | tf_op jit(solution)/shard_map/all_gather | solution.py:1062
  12.4 104.6 %all-gather.4.cloned.1.call-start = ((), (), s32[]{:S(2)}) async-start(), calls=%async_computation.3 | async-start | bytes 4386816 | tf_op jit(solution)/shard_map/all_gather | solution.py:1067
  13.1 8.5 %collective-permute-start.3 = (bf16[32,256]{1,0:T(8,128)(2,1)S(1)}, bf16[32,256]{1,0:T(8,128)(2,1)S(1)}, u32[]{:S(2)}, u32[]{:S(2)}) collective-permute-start(bf16[32,256]{1,0:T(8,128)(2,1)S(1)} %reshape.109), channel_id=1, source_target_pairs={{0,3},{1,0},{2,1},{3,2},{4,7},{5,4},{6,5},{7,6},{8,11},{9,8},{10,9... | collective-permute-start | bytes 49160 | tf_op jit(solution)/shard_map/ppermute | solution.py:941
  28.7 10.5 %collective-permute-start.12 = (bf16[48,768]{1,0:T(8,128)(2,1)S(1)}, bf16[48,768]{1,0:T(8,128)(2,1)S(1)}, u32[]{:S(2)}, u32[]{:S(2)}) collective-permute-start(bf16[48,768]{1,0:T(8,128)(2,1)S(1)} %slice.98), channel_id=1, source_target_pairs={{0,16},{4,20},{8,24},{12,28},{16,32},{20,36},{24,40},{28,44},{32,4... | collective-permute-start | bytes 221192 | tf_op jit(solution)/shard_map/ppermute | solution.py:964
  28.7 10.4 %collective-permute-start.11 = (bf16[48,1536]{1,0:T(8,128)(2,1)S(1)}, bf16[48,1536]{1,0:T(8,128)(2,1)S(1)}, u32[]{:S(2)}, u32[]{:S(2)}) collective-permute-start(bf16[48,1536]{1,0:T(8,128)(2,1)S(1)} %slice.97), channel_id=1, source_target_pairs={{0,48},{4,52},{8,56},{12,60},{16,0},{20,4},{24,8},{28,12},{32,16},... | collective-permute-start | bytes 442376 | tf_op jit(solution)/shard_map/ppermute | solution.py:964
  39.3 15.1 %collective-permute-start.14 = (bf16[192,2688]{1,0:T(8,128)(2,1)S(1)}, bf16[192,2688]{1,0:T(8,128)(2,1)S(1)}, u32[]{:S(2)}, u32[]{:S(2)}) collective-permute-start(bf16[192,2688]{1,0:T(8,128)(2,1)S(1)} %maximum_maximum_fusion.refs_2_.refs_6_), channel_id=1, source_target_pairs={{0,12},{4,0},{8,4},{12,8},{16,28},{20,16},{24,20},{28,24},{32,44},... | collective-permute-start | bytes 3096584 | tf_op jit(solution)/shard_map/ppermute | solution.py:964
  42.3 15.8 %collective-permute-start.15 = (bf16[192,2688]{1,0:T(8,128)(2,1)S(1)}, bf16[192,2688]{1,0:T(8,128)(2,1)S(1)}, u32[]{:S(2)}, u32[]{:S(2)}) collective-permute-start(bf16[192,2688]{1,0:T(8,128)(2,1)S(1)} %maximum_maximum_fusion.refs_2_.refs_6_), channel_id=1, source_target_pairs={{0,4},{4,8},{8,12},{12,0},{16,20},{20,24},{24,28},{28,16},{32,36},... | collective-permute-start | bytes 3096584 | tf_op jit(solution)/shard_map/ppermute | solution.py:964
  58.1 10.1 %collective-permute-start.16 = (bf16[192,1536]{1,0:T(8,128)(2,1)S(1)}, bf16[192,1536]{1,0:T(8,128)(2,1)}, u32[]{:S(2)}, u32[]{:S(2)}) collective-permute-start(bf16[192,1536]{1,0:T(8,128)(2,1)S(1)} %slice.99), channel_id=1, source_target_pairs={{0,12},{4,0},{8,4},{12,8},{16,28},{20,16},{24,20},{28,24},{32,44},... | collective-permute-start | bytes 1769480 | tf_op jit(solution)/shard_map/ppermute | solution.py:964
  58.3 9.7 %collective-permute-start.17 = (bf16[192,1152]{1,0:T(8,128)(2,1)S(1)}, bf16[192,1152]{1,0:T(8,128)(2,1)}, u32[]{:S(2)}, u32[]{:S(2)}) collective-permute-start(bf16[192,1152]{1,0:T(8,128)(2,1)S(1)} %slice.100), channel_id=1, source_target_pairs={{0,4},{4,8},{8,12},{12,0},{16,20},{20,24},{24,28},{28,16},{32,36},... | collective-permute-start | bytes 1327112 | tf_op jit(solution)/shard_map/ppermute | solution.py:964
  68.2 133.7 %reduce-scatter.6.cloned.1.call-start = ((), (), s32[]{:S(2)}) async-start(), calls=%async_computation.4 | async-start | bytes 1966080 | tf_op jit(solution)/shard_map/reduce_scatter | solution.py:1084
  93.8 13.9 %collective-permute-start.23 = (bf16[128,1664]{1,0:T(8,128)(2,1)}, bf16[128,1664]{1,0:T(8,128)(2,1)S(1)}, u32[]{:S(2)}, u32[]{:S(2)}) collective-permute-start(bf16[128,1664]{1,0:T(8,128)(2,1)} %get-tuple-element.138), channel_id=1, source_target_pairs={{0,1},{1,2},{2,3},{3,0},{4,5},{5,6},{6,7},{7,4},{8,9},{9,10},{10,1... | collective-permute-start | bytes 1277960 | tf_op jit(solution)/shard_map/ppermute | solution.py:941
  96.1 12.9 %collective-permute-start.24 = (bf16[128,1664]{1,0:T(8,128)(2,1)}, bf16[128,1664]{1,0:T(8,128)(2,1)S(1)}, u32[]{:S(2)}, u32[]{:S(2)}) collective-permute-start(bf16[128,1664]{1,0:T(8,128)(2,1)} %get-tuple-element.139), channel_id=1, source_target_pairs={{0,3},{1,0},{2,1},{3,2},{4,7},{5,4},{6,5},{7,6},{8,11},{9,8},{10,9... | collective-permute-start | bytes 1277960 | tf_op jit(solution)/shard_map/ppermute | solution.py:941
  97.2 19.4 %collective-permute-start.25 = (bf16[128,1664]{1,0:T(8,128)(2,1)}, bf16[128,1664]{1,0:T(8,128)(2,1)S(1)}, u32[]{:S(2)}, u32[]{:S(2)}) collective-permute-start(bf16[128,1664]{1,0:T(8,128)(2,1)} %get-tuple-element.140), channel_id=1, source_target_pairs={{0,2},{1,3},{2,0},{3,1},{4,6},{5,7},{6,4},{7,5},{8,10},{9,11},{10,... | collective-permute-start | bytes 1277960 | tf_op jit(solution)/shard_map/ppermute | solution.py:941
  117.0 9.2 %collective-permute-start.29 = (bf16[768,2688]{1,0:T(8,128)(2,1)}, bf16[768,2688]{1,0:T(8,128)(2,1)}, u32[]{:S(2)}, u32[]{:S(2)}) collective-permute-start(bf16[768,2688]{1,0:T(8,128)(2,1)} %all-gather.4.cloned.1.call-done.refs_6_), channel_id=1, source_target_pairs={{0,64},{64,0},{1,65},{65,1},{2,66},{66,2},{3,67},{67,3},{4,68},{68... | collective-permute-start | bytes 12386312 | tf_op jit(solution)/shard_map/ppermute | solution.py:937
  120.2 12.7 %collective-permute-start.26 = (bf16[128,1536]{1,0:T(8,128)(2,1)}, bf16[128,1536]{1,0:T(8,128)(2,1)S(1)}, u32[]{:S(2)}, u32[]{:S(2)}) collective-permute-start(bf16[128,1536]{1,0:T(8,128)(2,1)} %get-tuple-element.145.refs_2_.rows_ref), channel_id=1, source_target_pairs={{0,1},{1,2},{2,3},{3,0},{4,5},{5,6},{6,7},{7,4},{8,9},{9,10},{10,1... | collective-permute-start | bytes 1179656 | tf_op jit(solution)/shard_map/ppermute | solution.py:941
  121.5 12.2 %collective-permute-start.27 = (bf16[128,1536]{1,0:T(8,128)(2,1)}, bf16[128,1536]{1,0:T(8,128)(2,1)S(1)}, u32[]{:S(2)}, u32[]{:S(2)}) collective-permute-start(bf16[128,1536]{1,0:T(8,128)(2,1)} %get-tuple-element.145.refs_2_.rows_ref), channel_id=1, source_target_pairs={{0,3},{1,0},{2,1},{3,2},{4,7},{5,4},{6,5},{7,6},{8,11},{9,8},{10,9... | collective-permute-start | bytes 1179656 | tf_op jit(solution)/shard_map/ppermute | solution.py:941
  123.4 19.1 %collective-permute-start.28 = (bf16[128,1536]{1,0:T(8,128)(2,1)}, bf16[128,1536]{1,0:T(8,128)(2,1)S(1)}, u32[]{:S(2)}, u32[]{:S(2)}) collective-permute-start(bf16[128,1536]{1,0:T(8,128)(2,1)} %get-tuple-element.145.refs_2_.rows_ref), channel_id=1, source_target_pairs={{0,2},{1,3},{2,0},{3,1},{4,6},{5,7},{6,4},{7,5},{8,10},{9,11},{10,... | collective-permute-start | bytes 1179656 | tf_op jit(solution)/shard_map/ppermute | solution.py:941
  163.0 146.1 %reduce-scatter.10.cloned.1.call-start = ((), (), s32[]{:S(2)}) async-start(), calls=%async_computation.7 | async-start | bytes 4386816
  202.0 21.4 %collective-permute-start.34 = (bf16[128,1536]{1,0:T(8,128)(2,1)}, bf16[128,1536]{1,0:T(8,128)(2,1)S(1)}, u32[]{:S(2)}, u32[]{:S(2)}) collective-permute-start(bf16[128,1536]{1,0:T(8,128)(2,1)} %get-tuple-element.168), channel_id=1, source_target_pairs={{0,1},{1,2},{2,3},{3,0},{4,5},{5,6},{6,7},{7,4},{8,9},{9,10},{10,1... | collective-permute-start | bytes 1179656 | tf_op jit(solution)/shard_map/ppermute | solution.py:941
  202.1 21.3 %collective-permute-start.35 = (bf16[128,1536]{1,0:T(8,128)(2,1)}, bf16[128,1536]{1,0:T(8,128)(2,1)S(1)}, u32[]{:S(2)}, u32[]{:S(2)}) collective-permute-start(bf16[128,1536]{1,0:T(8,128)(2,1)} %get-tuple-element.169), channel_id=1, source_target_pairs={{0,3},{1,0},{2,1},{3,2},{4,7},{5,4},{6,5},{7,6},{8,11},{9,8},{10,9... | collective-permute-start | bytes 1179656 | tf_op jit(solution)/shard_map/ppermute | solution.py:941
  205.3 18.1 %collective-permute-start.36 = (bf16[128,1536]{1,0:T(8,128)(2,1)}, bf16[128,1536]{1,0:T(8,128)(2,1)S(1)}, u32[]{:S(2)}, u32[]{:S(2)}) collective-permute-start(bf16[128,1536]{1,0:T(8,128)(2,1)} %get-tuple-element.170), channel_id=1, source_target_pairs={{0,2},{1,3},{2,0},{3,1},{4,6},{5,7},{6,4},{7,5},{8,10},{9,11},{10,... | collective-permute-start | bytes 1179656 | tf_op jit(solution)/shard_map/ppermute | solution.py:941
  227.7 105.8 %reduce-scatter.8.cloned.1.call-start = ((), (), s32[]{:S(2)}) async-start(), calls=%async_computation.5 | async-start | bytes 1966080 | tf_op jit(solution)/shard_map/reduce_scatter | solution.py:1105
  228.7 13.5 %collective-permute-start.37 = (bf16[128,1664]{1,0:T(8,128)(2,1)S(1)}, bf16[128,1664]{1,0:T(8,128)(2,1)S(1)}, u32[]{:S(2)}, u32[]{:S(2)}) collective-permute-start(bf16[128,1664]{1,0:T(8,128)(2,1)S(1)} %copy-done.16), channel_id=1, source_target_pairs={{0,1},{1,2},{2,3},{3,0},{4,5},{5,6},{6,7},{7,4},{8,9},{9,10},{10,1... | collective-permute-start | bytes 1277960 | tf_op jit(solution)/shard_map/ppermute | solution.py:941
  229.3 20.4 %collective-permute-start.38 = (bf16[128,1664]{1,0:T(8,128)(2,1)S(1)}, bf16[128,1664]{1,0:T(8,128)(2,1)S(1)}, u32[]{:S(2)}, u32[]{:S(2)}) collective-permute-start(bf16[128,1664]{1,0:T(8,128)(2,1)S(1)} %copy-done.16), channel_id=1, source_target_pairs={{0,3},{1,0},{2,1},{3,2},{4,7},{5,4},{6,5},{7,6},{8,11},{9,8},{10,9... | collective-permute-start | bytes 1277960 | tf_op jit(solution)/shard_map/ppermute | solution.py:941
  231.9 19.2 %collective-permute-start.39 = (bf16[128,1664]{1,0:T(8,128)(2,1)S(1)}, bf16[128,1664]{1,0:T(8,128)(2,1)S(1)}, u32[]{:S(2)}, u32[]{:S(2)}) collective-permute-start(bf16[128,1664]{1,0:T(8,128)(2,1)S(1)} %copy-done.16), channel_id=1, source_target_pairs={{0,2},{1,3},{2,0},{3,1},{4,6},{5,7},{6,4},{7,5},{8,10},{9,11},{10,... | collective-permute-start | bytes 1277960 | tf_op jit(solution)/shard_map/ppermute | solution.py:941
  295.4 13.4 %collective-permute-start.41 = (bf16[192,1536]{1,0:T(8,128)(2,1)S(1)}, bf16[192,1536]{1,0:T(8,128)(2,1)S(1)}, u32[]{:S(2)}, u32[]{:S(2)}) collective-permute-start(bf16[192,1536]{1,0:T(8,128)(2,1)S(1)} %get-tuple-element.199), channel_id=1, source_target_pairs={{0,16},{4,20},{8,24},{12,28},{16,32},{20,36},{24,40},{28,44},{32,4... | collective-permute-start | bytes 1769480 | tf_op jit(solution)/shard_map/ppermute | solution.py:964
  296.8 9.7 %collective-permute-start.42 = (bf16[192,1152]{1,0:T(8,128)(2,1)S(1)}, bf16[192,1152]{1,0:T(8,128)(2,1)S(1)}, u32[]{:S(2)}, u32[]{:S(2)}) collective-permute-start(bf16[192,1152]{1,0:T(8,128)(2,1)S(1)} %get-tuple-element.200), channel_id=1, source_target_pairs={{0,48},{4,52},{8,56},{12,60},{16,0},{20,4},{24,8},{28,12},{32,16},... | collective-permute-start | bytes 1327112 | tf_op jit(solution)/shard_map/ppermute | solution.py:964
  309.0 15.9 %collective-permute-start.43 = (bf16[192,2688]{1,0:T(8,128)(2,1)S(1)}, bf16[192,2688]{1,0:T(8,128)(2,1)S(1)}, u32[]{:S(2)}, u32[]{:S(2)}) collective-permute-start(bf16[192,2688]{1,0:T(8,128)(2,1)S(1)} %get-tuple-element.205), channel_id=1, source_target_pairs={{0,16},{4,20},{8,24},{12,28},{16,32},{20,36},{24,40},{28,44},{32,4... | collective-permute-start | bytes 3096584 | tf_op jit(solution)/shard_map/ppermute | solution.py:964
  309.1 15.8 %collective-permute-start.44 = (bf16[192,2688]{1,0:T(8,128)(2,1)S(1)}, bf16[192,2688]{1,0:T(8,128)(2,1)S(1)}, u32[]{:S(2)}, u32[]{:S(2)}) collective-permute-start(bf16[192,2688]{1,0:T(8,128)(2,1)S(1)} %get-tuple-element.206), channel_id=1, source_target_pairs={{0,48},{4,52},{8,56},{12,60},{16,0},{20,4},{24,8},{28,12},{32,16},... | collective-permute-start | bytes 3096584 | tf_op jit(solution)/shard_map/ppermute | solution.py:964
  345.3 9.8 %collective-permute-start.47 = (f32[128,1536]{1,0:T(8,128)}, f32[128,1536]{1,0:T(8,128)}, u32[]{:S(2)}, u32[]{:S(2)}) collective-permute-start(f32[128,1536]{1,0:T(8,128)} %broadcast_select_fusion), channel_id=1, source_target_pairs={{0,64},{64,0},{1,65},{65,1},{2,66},{66,2},{3,67},{67,3},{4,68},{68... | collective-permute-start | bytes 2359304 | tf_op jit(solution)/shard_map/ppermute | solution.py:937
  348.3 9.6 %collective-permute-start.51 = (f32[32,256]{1,0:T(8,128)S(1)}, f32[32,256]{1,0:T(8,128)S(1)}, u32[]{:S(2)}, u32[]{:S(2)}) collective-permute-start(f32[32,256]{1,0:T(8,128)S(1)} %get-tuple-element.266), channel_id=1, source_target_pairs={{0,1},{1,2},{2,3},{3,0},{4,5},{5,6},{6,7},{7,4},{8,9},{9,10},{10,1... | collective-permute-start | bytes 98312 | tf_op jit(solution)/shard_map/ppermute | solution.py:941
  348.6 9.3 %collective-permute-start.52 = (f32[32,256]{1,0:T(8,128)S(1)}, f32[32,256]{1,0:T(8,128)S(1)}, u32[]{:S(2)}, u32[]{:S(2)}) collective-permute-start(f32[32,256]{1,0:T(8,128)S(1)} %get-tuple-element.265), channel_id=1, source_target_pairs={{0,3},{1,0},{2,1},{3,2},{4,7},{5,4},{6,5},{7,6},{8,11},{9,8},{10,9... | collective-permute-start | bytes 98312 | tf_op jit(solution)/shard_map/ppermute | solution.py:941
  (75 other events, 539.2 us)
Sparse Core Ops, SparseCore 0:
  12.6 42.3 all-gather.5
  68.3 48.6 all-gather.3
  163.1 24.3 reduce-scatter.5
  227.8 78.1 reduce-scatter.9
  309.2 24.2 reduce-scatter.7

commit v2 on v1

--- a/solution.py
+++ b/solution.py
@@ -79,7 +79,7 @@
 
 
 def sigmoid(v):
-    return 1.0 / (1.0 + jnp.exp(-v))
+    return 0.5 * jnp.tanh(0.5 * v) + 0.5
 
 
 def softplus(v):
@@ -835,7 +835,11 @@
     )(where, misc, heads)
 
 
-def both_kernel(where_ref, mine, given, *outs):
+def both_kernel(where_ref, mine_in, given, *refs):
+    outs, mine, sem = refs[:-2], refs[-2], refs[-1]
+    load = pltpu.make_async_copy(mine_in, mine, sem)
+    load.start()
+    load.wait()
     if len(outs) == 1:
         outs[0][...] = (mine[...].astype(F32) + given[...].astype(F32)).astype(BF)
         return
@@ -867,9 +871,10 @@
     return pl.pallas_call(
         both_kernel,
         out_shape=out_shape,
-        in_specs=[SMEM] + [VMEM] * 2,
+        in_specs=[SMEM, HBM, VMEM],
         out_specs=[VMEM] * len(out_shape),
-        scratch_shapes=[pltpu.VMEM((4, 192, WIDE), BF)] if relative else [],
+        scratch_shapes=([pltpu.VMEM((4, 192, WIDE), BF)] if relative else [])
+        + [pltpu.VMEM((SIDE, WIDE), BF), pltpu.SemaphoreType.DMA],
         compiler_params=limit(28),
         cost_estimate=cost(10**6, 10**4),
         name="both_cores_grads",

time: 376 us -> 376 us (level)
  no operation moved by 1% of the time
where the time goes in v2:
time: 376 us; the launch traced here: 368 us
  waiting for transfers between devices  137 us (36%)
  Pallas kernels  118 us (31%)
  starting transfers between devices  61.7 us (16%)
  local copies, waits for them, and re-layouts  28.6 us (8%)
  between operations  15.1 us (4%)
  other arithmetic  7.91 us (2%)
    pallas_call x2, Pallas kernels, backward_call(): pl.pallas_call(kernel, out_shape=out_shape, in_specs=in_specs, out_specs=...  60.4 us
    ppermute x21, waiting for transfers between devices, turn(): return lax.ppermute(v, axis, [(i, (i + by) % 4) for i in range(4)])  60.1 us
    ppermute x19, waiting for transfers between devices, ring(): return lax.ppermute(v, ('section', *DP), pairs)  58.3 us
    pallas_call x2, Pallas kernels, forward_call(): pl.pallas_call(kernel, out_shape=out_shape, in_specs=in_specs, out_specs=...  36.7 us
    ppermute x21, starting transfers between devices, turn(): return lax.ppermute(v, axis, [(i, (i + by) % 4) for i in range(4)])  29.7 us
    ppermute x19, starting transfers between devices, ring(): return lax.ppermute(v, ('section', *DP), pairs)  27.8 us
    unnamed x113, local copies, waits for them, and re-layouts  17.5 us
    ppermute x14, waiting for transfers between devices, swap(): return lax.ppermute(v, 'section', [(0, 1), (1, 0)])  16.8 us
  transfers between devices with their start and end apart: 59, of which 35 were waited for; matrix products, arithmetic and copies ran while one was open for 5% of the time, Pallas kernels for 25%

profile of v2, /device:TPU:0, one launch (start us, length us, event | category | flops | bytes accessed | tf_op | source)
XLA Modules:
  0.0 368.1 jit_solution(466624124333141507)
XLA Ops:
  13.1 4.2 %collective-permute-start.3 = (bf16[32,256]{1,0:T(8,128)(2,1)S(1)}, bf16[32,256]{1,0:T(8,128)(2,1)S(1)}, u32[]{:S(2)}, u32[]{:S(2)}) collective-permute-start(bf16[32,256]{1,0:T(8,128)(2,1)S(1)} %reshape.109), channel_id=1, source_target_pairs={{0,3},{1,0},{2,1},{3,2},{4,7},{5,4},{6,5},{7,6},{8,11},{9,8},{10,9... | collective-permute-start | bytes 49160 | tf_op jit(solution)/shard_map/ppermute | solution.py:946
  18.5 3.0 collective-permute-start.8
  25.0 3.7 %collective-permute-done.9 = bf16[48,2304]{1,0:T(8,128)(2,1)S(1)} collective-permute-done((bf16[48,2304]{1,0:T(8,128)(2,1)S(1)}, bf16[48,2304]{1,0:T(8,128)(2,1)S(1)}, u32[]{:S(2)}, u32[]{:S(2)}) %collective-permute-start.9) | collective-permute-done | bytes 221216 | tf_op jit(solution)/shard_map/ppermute | solution.py:969
  28.7 3.3 collective-permute-start.11
  39.3 3.0 collective-permute-start.14
  42.3 12.1 %collective-permute-done.14.refs_3_.refs_7_ = bf16[192,2688]{1,0:T(8,128)(2,1)S(1)} collective-permute-done((bf16[192,2688]{1,0:T(8,128)(2,1)S(1)}, bf16[192,2688]{1,0:T(8,128)(2,1)S(1)}, u32[]{:S(2)}, u32[]{:S(2)}) %collective-permute-start.14) | collective-permute-done | bytes 1032224 | tf_op jit(solution)/shard_map/ppermute | solution.py:969
  54.4 3.7 %collective-permute-done.15.refs_6_.refs_10_ = bf16[192,2688]{1,0:T(8,128)(2,1)S(1)} collective-permute-done((bf16[192,2688]{1,0:T(8,128)(2,1)S(1)}, bf16[192,2688]{1,0:T(8,128)(2,1)S(1)}, u32[]{:S(2)}, u32[]{:S(2)}) %collective-permute-start.15) | collective-permute-done | bytes 1032224 | tf_op jit(solution)/shard_map/ppermute | solution.py:969
  61.7 6.3 %collective-permute-done.17.refs_5_.refs_9_ = bf16[192,1152]{1,0:T(8,128)(2,1)} collective-permute-done((bf16[192,1152]{1,0:T(8,128)(2,1)S(1)}, bf16[192,1152]{1,0:T(8,128)(2,1)}, u32[]{:S(2)}, u32[]{:S(2)}) %collective-permute-start.17) | collective-permute-done | bytes 442400 | tf_op jit(solution)/shard_map/ppermute | solution.py:969
  70.2 5.4 %collective-permute-done.21.refs_10_.refs_14_ = bf16[192,1152]{1,0:T(8,128)(2,1)S(1)} collective-permute-done((bf16[192,1152]{1,0:T(8,128)(2,1)}, bf16[192,1152]{1,0:T(8,128)(2,1)S(1)}, u32[]{:S(2)}, u32[]{:S(2)}) %collective-permute-start.21) | collective-permute-done | bytes 442400 | tf_op jit(solution)/shard_map/ppermute | solution.py:942
  76.6 17.1 %layer_forward.2 = (bf16[512,1536]{1,0:T(8,128)(2,1)}, f32[512,1920]{1,0:T(8,128)}, f32[512,768]{1,0:T(8,128)}, bf16[4,128,768]{2,1,0:T(8,128)(2,1)}, bf16[512,7...) custom-call(s32[4]{0:T(128)} %pad_add_fusion.refs_0_.where_ref, ...), custom_call_target="tpu_custom_call" | custom-call | flops 20000000000 | bytes 24000000 | tf_op jit(solution)/shard_map/layer_forward/pallas_call | solution.py:425
  98.1 9.6 %collective-permute-done.23.b = bf16[128,1664]{1,0:T(8,128)(2,1)S(1)} collective-permute-done((bf16[128,1664]{1,0:T(8,128)(2,1)}, bf16[128,1664]{1,0:T(8,128)(2,1)S(1)}, u32[]{:S(2)}, u32[]{:S(2)}) %collective-permute-start.23) | collective-permute-done | bytes 426016 | tf_op jit(solution)/shard_map/ppermute | solution.py:946
  108.9 7.5 %collective-permute-done.25.d = bf16[128,1664]{1,0:T(8,128)(2,1)S(1)} collective-permute-done((bf16[128,1664]{1,0:T(8,128)(2,1)}, bf16[128,1664]{1,0:T(8,128)(2,1)S(1)}, u32[]{:S(2)}, u32[]{:S(2)}) %collective-permute-start.25) | collective-permute-done | bytes 426016 | tf_op jit(solution)/shard_map/ppermute | solution.py:946
  117.2 2.9 between_layers.1
  133.7 8.8 %collective-permute-done.28.refs_5_ = bf16[128,1536]{1,0:T(8,128)(2,1)S(1)} collective-permute-done((bf16[128,1536]{1,0:T(8,128)(2,1)}, bf16[128,1536]{1,0:T(8,128)(2,1)S(1)}, u32[]{:S(2)}, u32[]{:S(2)}) %collective-permute-start.28) | collective-permute-done | bytes 393248 | tf_op jit(solution)/shard_map/ppermute | solution.py:946
  143.3 19.6 %layer_forward.3 = (bf16[512,1536]{1,0:T(8,128)(2,1)}, f32[512,1920]{1,0:T(8,128)}, f32[512,768]{1,0:T(8,128)}, bf16[4,128,768]{2,1,0:T(8,128)(2,1)}, bf16[512,7...) custom-call(s32[4]{0:T(128)} %pad_add_fusion.refs_0_.where_ref, ...), custom_call_target="tpu_custom_call" | custom-call | flops 20000000000 | bytes 24000000 | tf_op jit(solution)/shard_map/layer_forward/pallas_call | solution.py:425
  168.2 3.5 collective-permute-done.32.refs_17_.d
  172.3 29.5 %layer_backward.2 = (bf16[128,1536]{1,0:T(8,128)(2,1)}, bf16[128,1536]{1,0:T(8,128)(2,1)}, bf16[128,1536]{1,0:T(8,128)(2,1)}, bf16[128,1536]{1,0:T(8,128)(2,1)},...) custom-call(s32[4]{0:T(128)} %pad_add_fusion.refs_0_.where_ref, ...), custom_call_target="tpu_custom_call" | custom-call | flops 32000000000 | bytes 30000000 | tf_op jit(solution)/shard_map/layer_backward/pallas_call | solution.py:720
  202.0 3.2 collective-permute-start.35
  205.2 4.0 %collective-permute-done.33.given = bf16[768,2688]{1,0:T(8,128)(2,1)S(1)} collective-permute-done((bf16[768,2688]{1,0:T(8,128)(2,1)}, bf16[768,2688]{1,0:T(8,128)(2,1)S(1)}, u32[]{:S(2)}, u32[]{:S(2)}) %collective-permute-start.33) | collective-permute-done | bytes 4128800 | tf_op jit(solution)/shard_map/ppermute | solution.py:942
  215.5 7.8 %collective-permute-done.34.b = bf16[128,1536]{1,0:T(8,128)(2,1)S(1)} collective-permute-done((bf16[128,1536]{1,0:T(8,128)(2,1)}, bf16[128,1536]{1,0:T(8,128)(2,1)S(1)}, u32[]{:S(2)}, u32[]{:S(2)}) %collective-permute-start.34) | collective-permute-done | bytes 393248 | tf_op jit(solution)/shard_map/ppermute | solution.py:946
  224.3 3.3 between_layers_back.1.refs_20_.grad_ref
  229.2 2.6 collective-permute-start.38
  235.2 6.9 %collective-permute-done.37.refs_21_ = bf16[128,1664]{1,0:T(8,128)(2,1)S(1)} collective-permute-done((bf16[128,1664]{1,0:T(8,128)(2,1)S(1)}, bf16[128,1664]{1,0:T(8,128)(2,1)S(1)}, u32[]{:S(2)}, u32[]{:S(2)}) %collective-permute-start.37) | collective-permute-done | bytes 426016 | tf_op jit(solution)/shard_map/ppermute | solution.py:946
  242.1 7.5 %collective-permute-done.38.refs_22_ = bf16[128,1664]{1,0:T(8,128)(2,1)S(1)} collective-permute-done((bf16[128,1664]{1,0:T(8,128)(2,1)S(1)}, bf16[128,1664]{1,0:T(8,128)(2,1)S(1)}, u32[]{:S(2)}, u32[]{:S(2)}) %collective-permute-start.38) | collective-permute-done | bytes 426016 | tf_op jit(solution)/shard_map/ppermute | solution.py:946
  251.8 30.9 %layer_backward.3 = (bf16[512,1536]{1,0:T(8,128)(2,1)}, f32[16,1536]{1,0:T(8,128)}, bf16[768,2688]{1,0:T(8,128)(2,1)}, bf16[768,2688]{1,0:T(8,128)(2,1)}) custom-call(s32[4]{0:T(128)} %pad_add_fusion.refs_0_.where_ref, bf16[512,1536]{1,0:T(8,128)(2,1)} %get-tuple-element.180.refs_1_, f32[512,1920]{1,0:T(8,128)} %get-tuple-element.181.refs_2_, ...), custom_call_target="tpu_custom_call" | custom-call | flops 32000000000 | bytes 30000000 | tf_op jit(solution)/shard_map/layer_backward/pallas_call | solution.py:720
  282.8 7.3 %collective-permute-done.40.given = bf16[768,2688]{1,0:T(8,128)(2,1)S(1)} collective-permute-done((bf16[768,2688]{1,0:T(8,128)(2,1)}, bf16[768,2688]{1,0:T(8,128)(2,1)S(1)}, u32[]{:S(2)}, u32[]{:S(2)}) %collective-permute-start.40) | collective-permute-done | bytes 4128800 | tf_op jit(solution)/shard_map/ppermute | solution.py:942
  292.3 3.3 both_cores_grads.3
  298.9 7.6 %collective-permute-done.42.right = bf16[192,1152]{1,0:T(8,128)(2,1)S(1)} collective-permute-done((bf16[192,1152]{1,0:T(8,128)(2,1)S(1)}, bf16[192,1152]{1,0:T(8,128)(2,1)S(1)}, u32[]{:S(2)}, u32[]{:S(2)}) %collective-permute-start.42) | collective-permute-done | bytes 442400 | tf_op jit(solution)/shard_map/ppermute | solution.py:969
  309.0 3.2 collective-permute-start.44
  312.3 12.6 %collective-permute-done.43.b = bf16[192,2688]{1,0:T(8,128)(2,1)S(1)} collective-permute-done((bf16[192,2688]{1,0:T(8,128)(2,1)S(1)}, bf16[192,2688]{1,0:T(8,128)(2,1)S(1)}, u32[]{:S(2)}, u32[]{:S(2)}) %collective-permute-start.43) | collective-permute-done | bytes 1032224 | tf_op jit(solution)/shard_map/ppermute | solution.py:969
  348.6 2.7 collective-permute-start.52
  355.0 2.7 maximum_select_fusion
  (299 shorter events, 104.3 us)
Async XLA Ops:
  7.2 68.6 %all-gather.6.cloned.1.call-start = ((), (), s32[]{:S(2)}) async-start(), calls=%async_computation.6 | async-start | bytes 3932160 | tf_op jit(solution)/shard_map/all_gather | solution.py:1067
  12.4 104.6 %all-gather.4.cloned.1.call-start = ((), (), s32[]{:S(2)}) async-start(), calls=%async_computation.3 | async-start | bytes 4386816 | tf_op jit(solution)/shard_map/all_gather | solution.py:1072
  13.1 8.5 %collective-permute-start.3 = (bf16[32,256]{1,0:T(8,128)(2,1)S(1)}, bf16[32,256]{1,0:T(8,128)(2,1)S(1)}, u32[]{:S(2)}, u32[]{:S(2)}) collective-permute-start(bf16[32,256]{1,0:T(8,128)(2,1)S(1)} %reshape.109), channel_id=1, source_target_pairs={{0,3},{1,0},{2,1},{3,2},{4,7},{5,4},{6,5},{7,6},{8,11},{9,8},{10,9... | collective-permute-start | bytes 49160 | tf_op jit(solution)/shard_map/ppermute | solution.py:946
  28.7 10.5 %collective-permute-start.12 = (bf16[48,768]{1,0:T(8,128)(2,1)S(1)}, bf16[48,768]{1,0:T(8,128)(2,1)S(1)}, u32[]{:S(2)}, u32[]{:S(2)}) collective-permute-start(bf16[48,768]{1,0:T(8,128)(2,1)S(1)} %slice.98), channel_id=1, source_target_pairs={{0,16},{4,20},{8,24},{12,28},{16,32},{20,36},{24,40},{28,44},{32,4... | collective-permute-start | bytes 221192 | tf_op jit(solution)/shard_map/ppermute | solution.py:969
  28.7 10.4 %collective-permute-start.11 = (bf16[48,1536]{1,0:T(8,128)(2,1)S(1)}, bf16[48,1536]{1,0:T(8,128)(2,1)S(1)}, u32[]{:S(2)}, u32[]{:S(2)}) collective-permute-start(bf16[48,1536]{1,0:T(8,128)(2,1)S(1)} %slice.97), channel_id=1, source_target_pairs={{0,48},{4,52},{8,56},{12,60},{16,0},{20,4},{24,8},{28,12},{32,16},... | collective-permute-start | bytes 442376 | tf_op jit(solution)/shard_map/ppermute | solution.py:969
  39.3 15.1 %collective-permute-start.14 = (bf16[192,2688]{1,0:T(8,128)(2,1)S(1)}, bf16[192,2688]{1,0:T(8,128)(2,1)S(1)}, u32[]{:S(2)}, u32[]{:S(2)}) collective-permute-start(bf16[192,2688]{1,0:T(8,128)(2,1)S(1)} %maximum_maximum_fusion.refs_2_.refs_6_), channel_id=1, source_target_pairs={{0,12},{4,0},{8,4},{12,8},{16,28},{20,16},{24,20},{28,24},{32,44},... | collective-permute-start | bytes 3096584 | tf_op jit(solution)/shard_map/ppermute | solution.py:969
  42.3 15.8 %collective-permute-start.15 = (bf16[192,2688]{1,0:T(8,128)(2,1)S(1)}, bf16[192,2688]{1,0:T(8,128)(2,1)S(1)}, u32[]{:S(2)}, u32[]{:S(2)}) collective-permute-start(bf16[192,2688]{1,0:T(8,128)(2,1)S(1)} %maximum_maximum_fusion.refs_2_.refs_6_), channel_id=1, source_target_pairs={{0,4},{4,8},{8,12},{12,0},{16,20},{20,24},{24,28},{28,16},{32,36},... | collective-permute-start | bytes 3096584 | tf_op jit(solution)/shard_map/ppermute | solution.py:969
  58.1 10.1 %collective-permute-start.16 = (bf16[192,1536]{1,0:T(8,128)(2,1)S(1)}, bf16[192,1536]{1,0:T(8,128)(2,1)}, u32[]{:S(2)}, u32[]{:S(2)}) collective-permute-start(bf16[192,1536]{1,0:T(8,128)(2,1)S(1)} %slice.99), channel_id=1, source_target_pairs={{0,12},{4,0},{8,4},{12,8},{16,28},{20,16},{24,20},{28,24},{32,44},... | collective-permute-start | bytes 1769480 | tf_op jit(solution)/shard_map/ppermute | solution.py:969
  58.3 9.7 %collective-permute-start.17 = (bf16[192,1152]{1,0:T(8,128)(2,1)S(1)}, bf16[192,1152]{1,0:T(8,128)(2,1)}, u32[]{:S(2)}, u32[]{:S(2)}) collective-permute-start(bf16[192,1152]{1,0:T(8,128)(2,1)S(1)} %slice.100), channel_id=1, source_target_pairs={{0,4},{4,8},{8,12},{12,0},{16,20},{20,24},{24,28},{28,16},{32,36},... | collective-permute-start | bytes 1327112 | tf_op jit(solution)/shard_map/ppermute | solution.py:969
  68.2 133.6 %reduce-scatter.6.cloned.1.call-start = ((), (), s32[]{:S(2)}) async-start(), calls=%async_computation.4 | async-start | bytes 1966080 | tf_op jit(solution)/shard_map/reduce_scatter | solution.py:1089
  93.7 13.9 %collective-permute-start.23 = (bf16[128,1664]{1,0:T(8,128)(2,1)}, bf16[128,1664]{1,0:T(8,128)(2,1)S(1)}, u32[]{:S(2)}, u32[]{:S(2)}) collective-permute-start(bf16[128,1664]{1,0:T(8,128)(2,1)} %get-tuple-element.138), channel_id=1, source_target_pairs={{0,1},{1,2},{2,3},{3,0},{4,5},{5,6},{6,7},{7,4},{8,9},{9,10},{10,1... | collective-permute-start | bytes 1277960 | tf_op jit(solution)/shard_map/ppermute | solution.py:946
  95.9 12.9 %collective-permute-start.24 = (bf16[128,1664]{1,0:T(8,128)(2,1)}, bf16[128,1664]{1,0:T(8,128)(2,1)S(1)}, u32[]{:S(2)}, u32[]{:S(2)}) collective-permute-start(bf16[128,1664]{1,0:T(8,128)(2,1)} %get-tuple-element.139), channel_id=1, source_target_pairs={{0,3},{1,0},{2,1},{3,2},{4,7},{5,4},{6,5},{7,6},{8,11},{9,8},{10,9... | collective-permute-start | bytes 1277960 | tf_op jit(solution)/shard_map/ppermute | solution.py:946
  97.0 19.4 %collective-permute-start.25 = (bf16[128,1664]{1,0:T(8,128)(2,1)}, bf16[128,1664]{1,0:T(8,128)(2,1)S(1)}, u32[]{:S(2)}, u32[]{:S(2)}) collective-permute-start(bf16[128,1664]{1,0:T(8,128)(2,1)} %get-tuple-element.140), channel_id=1, source_target_pairs={{0,2},{1,3},{2,0},{3,1},{4,6},{5,7},{6,4},{7,5},{8,10},{9,11},{10,... | collective-permute-start | bytes 1277960 | tf_op jit(solution)/shard_map/ppermute | solution.py:946
  117.0 9.2 %collective-permute-start.29 = (bf16[768,2688]{1,0:T(8,128)(2,1)}, bf16[768,2688]{1,0:T(8,128)(2,1)}, u32[]{:S(2)}, u32[]{:S(2)}) collective-permute-start(bf16[768,2688]{1,0:T(8,128)(2,1)} %all-gather.4.cloned.1.call-done.refs_6_), channel_id=1, source_target_pairs={{0,64},{64,0},{1,65},{65,1},{2,66},{66,2},{3,67},{67,3},{4,68},{68... | collective-permute-start | bytes 12386312 | tf_op jit(solution)/shard_map/ppermute | solution.py:942
  120.0 12.9 %collective-permute-start.26 = (bf16[128,1536]{1,0:T(8,128)(2,1)}, bf16[128,1536]{1,0:T(8,128)(2,1)S(1)}, u32[]{:S(2)}, u32[]{:S(2)}) collective-permute-start(bf16[128,1536]{1,0:T(8,128)(2,1)} %get-tuple-element.145.refs_2_.rows_ref), channel_id=1, source_target_pairs={{0,1},{1,2},{2,3},{3,0},{4,5},{5,6},{6,7},{7,4},{8,9},{9,10},{10,1... | collective-permute-start | bytes 1179656 | tf_op jit(solution)/shard_map/ppermute | solution.py:946
  121.5 12.2 %collective-permute-start.27 = (bf16[128,1536]{1,0:T(8,128)(2,1)}, bf16[128,1536]{1,0:T(8,128)(2,1)S(1)}, u32[]{:S(2)}, u32[]{:S(2)}) collective-permute-start(bf16[128,1536]{1,0:T(8,128)(2,1)} %get-tuple-element.145.refs_2_.rows_ref), channel_id=1, source_target_pairs={{0,3},{1,0},{2,1},{3,2},{4,7},{5,4},{6,5},{7,6},{8,11},{9,8},{10,9... | collective-permute-start | bytes 1179656 | tf_op jit(solution)/shard_map/ppermute | solution.py:946
  123.3 19.2 %collective-permute-start.28 = (bf16[128,1536]{1,0:T(8,128)(2,1)}, bf16[128,1536]{1,0:T(8,128)(2,1)S(1)}, u32[]{:S(2)}, u32[]{:S(2)}) collective-permute-start(bf16[128,1536]{1,0:T(8,128)(2,1)} %get-tuple-element.145.refs_2_.rows_ref), channel_id=1, source_target_pairs={{0,2},{1,3},{2,0},{3,1},{4,6},{5,7},{6,4},{7,5},{8,10},{9,11},{10,... | collective-permute-start | bytes 1179656 | tf_op jit(solution)/shard_map/ppermute | solution.py:946
  162.9 146.0 %reduce-scatter.10.cloned.1.call-start = ((), (), s32[]{:S(2)}) async-start(), calls=%async_computation.7 | async-start | bytes 4386816
  201.9 21.4 %collective-permute-start.34 = (bf16[128,1536]{1,0:T(8,128)(2,1)}, bf16[128,1536]{1,0:T(8,128)(2,1)S(1)}, u32[]{:S(2)}, u32[]{:S(2)}) collective-permute-start(bf16[128,1536]{1,0:T(8,128)(2,1)} %get-tuple-element.168), channel_id=1, source_target_pairs={{0,1},{1,2},{2,3},{3,0},{4,5},{5,6},{6,7},{7,4},{8,9},{9,10},{10,1... | collective-permute-start | bytes 1179656 | tf_op jit(solution)/shard_map/ppermute | solution.py:946
  202.0 21.3 %collective-permute-start.35 = (bf16[128,1536]{1,0:T(8,128)(2,1)}, bf16[128,1536]{1,0:T(8,128)(2,1)S(1)}, u32[]{:S(2)}, u32[]{:S(2)}) collective-permute-start(bf16[128,1536]{1,0:T(8,128)(2,1)} %get-tuple-element.169), channel_id=1, source_target_pairs={{0,3},{1,0},{2,1},{3,2},{4,7},{5,4},{6,5},{7,6},{8,11},{9,8},{10,9... | collective-permute-start | bytes 1179656 | tf_op jit(solution)/shard_map/ppermute | solution.py:946
  205.2 18.1 %collective-permute-start.36 = (bf16[128,1536]{1,0:T(8,128)(2,1)}, bf16[128,1536]{1,0:T(8,128)(2,1)S(1)}, u32[]{:S(2)}, u32[]{:S(2)}) collective-permute-start(bf16[128,1536]{1,0:T(8,128)(2,1)} %get-tuple-element.170), channel_id=1, source_target_pairs={{0,2},{1,3},{2,0},{3,1},{4,6},{5,7},{6,4},{7,5},{8,10},{9,11},{10,... | collective-permute-start | bytes 1179656 | tf_op jit(solution)/shard_map/ppermute | solution.py:946
  227.6 105.8 %reduce-scatter.8.cloned.1.call-start = ((), (), s32[]{:S(2)}) async-start(), calls=%async_computation.5 | async-start | bytes 1966080 | tf_op jit(solution)/shard_map/reduce_scatter | solution.py:1110
  228.6 13.5 %collective-permute-start.37 = (bf16[128,1664]{1,0:T(8,128)(2,1)S(1)}, bf16[128,1664]{1,0:T(8,128)(2,1)S(1)}, u32[]{:S(2)}, u32[]{:S(2)}) collective-permute-start(bf16[128,1664]{1,0:T(8,128)(2,1)S(1)} %copy-done.16), channel_id=1, source_target_pairs={{0,1},{1,2},{2,3},{3,0},{4,5},{5,6},{6,7},{7,4},{8,9},{9,10},{10,1... | collective-permute-start | bytes 1277960 | tf_op jit(solution)/shard_map/ppermute | solution.py:946
  229.2 20.4 %collective-permute-start.38 = (bf16[128,1664]{1,0:T(8,128)(2,1)S(1)}, bf16[128,1664]{1,0:T(8,128)(2,1)S(1)}, u32[]{:S(2)}, u32[]{:S(2)}) collective-permute-start(bf16[128,1664]{1,0:T(8,128)(2,1)S(1)} %copy-done.16), channel_id=1, source_target_pairs={{0,3},{1,0},{2,1},{3,2},{4,7},{5,4},{6,5},{7,6},{8,11},{9,8},{10,9... | collective-permute-start | bytes 1277960 | tf_op jit(solution)/shard_map/ppermute | solution.py:946
  231.8 19.2 %collective-permute-start.39 = (bf16[128,1664]{1,0:T(8,128)(2,1)S(1)}, bf16[128,1664]{1,0:T(8,128)(2,1)S(1)}, u32[]{:S(2)}, u32[]{:S(2)}) collective-permute-start(bf16[128,1664]{1,0:T(8,128)(2,1)S(1)} %copy-done.16), channel_id=1, source_target_pairs={{0,2},{1,3},{2,0},{3,1},{4,6},{5,7},{6,4},{7,5},{8,10},{9,11},{10,... | collective-permute-start | bytes 1277960 | tf_op jit(solution)/shard_map/ppermute | solution.py:946
  295.6 13.0 %collective-permute-start.41 = (bf16[192,1536]{1,0:T(8,128)(2,1)S(1)}, bf16[192,1536]{1,0:T(8,128)(2,1)S(1)}, u32[]{:S(2)}, u32[]{:S(2)}) collective-permute-start(bf16[192,1536]{1,0:T(8,128)(2,1)S(1)} %get-tuple-element.199), channel_id=1, source_target_pairs={{0,16},{4,20},{8,24},{12,28},{16,32},{20,36},{24,40},{28,44},{32,4... | collective-permute-start | bytes 1769480 | tf_op jit(solution)/shard_map/ppermute | solution.py:969
  297.0 9.5 %collective-permute-start.42 = (bf16[192,1152]{1,0:T(8,128)(2,1)S(1)}, bf16[192,1152]{1,0:T(8,128)(2,1)S(1)}, u32[]{:S(2)}, u32[]{:S(2)}) collective-permute-start(bf16[192,1152]{1,0:T(8,128)(2,1)S(1)} %get-tuple-element.200), channel_id=1, source_target_pairs={{0,48},{4,52},{8,56},{12,60},{16,0},{20,4},{24,8},{28,12},{32,16},... | collective-permute-start | bytes 1327112 | tf_op jit(solution)/shard_map/ppermute | solution.py:969
  309.0 15.9 %collective-permute-start.43 = (bf16[192,2688]{1,0:T(8,128)(2,1)S(1)}, bf16[192,2688]{1,0:T(8,128)(2,1)S(1)}, u32[]{:S(2)}, u32[]{:S(2)}) collective-permute-start(bf16[192,2688]{1,0:T(8,128)(2,1)S(1)} %get-tuple-element.205), channel_id=1, source_target_pairs={{0,16},{4,20},{8,24},{12,28},{16,32},{20,36},{24,40},{28,44},{32,4... | collective-permute-start | bytes 3096584 | tf_op jit(solution)/shard_map/ppermute | solution.py:969
  309.0 15.8 %collective-permute-start.44 = (bf16[192,2688]{1,0:T(8,128)(2,1)S(1)}, bf16[192,2688]{1,0:T(8,128)(2,1)S(1)}, u32[]{:S(2)}, u32[]{:S(2)}) collective-permute-start(bf16[192,2688]{1,0:T(8,128)(2,1)S(1)} %get-tuple-element.206), channel_id=1, source_target_pairs={{0,48},{4,52},{8,56},{12,60},{16,0},{20,4},{24,8},{28,12},{32,16},... | collective-permute-start | bytes 3096584 | tf_op jit(solution)/shard_map/ppermute | solution.py:969
  345.2 9.8 %collective-permute-start.47 = (f32[128,1536]{1,0:T(8,128)}, f32[128,1536]{1,0:T(8,128)}, u32[]{:S(2)}, u32[]{:S(2)}) collective-permute-start(f32[128,1536]{1,0:T(8,128)} %broadcast_select_fusion), channel_id=1, source_target_pairs={{0,64},{64,0},{1,65},{65,1},{2,66},{66,2},{3,67},{67,3},{4,68},{68... | collective-permute-start | bytes 2359304 | tf_op jit(solution)/shard_map/ppermute | solution.py:942
  348.1 9.6 %collective-permute-start.51 = (f32[32,256]{1,0:T(8,128)S(1)}, f32[32,256]{1,0:T(8,128)S(1)}, u32[]{:S(2)}, u32[]{:S(2)}) collective-permute-start(f32[32,256]{1,0:T(8,128)S(1)} %get-tuple-element.266), channel_id=1, source_target_pairs={{0,1},{1,2},{2,3},{3,0},{4,5},{5,6},{6,7},{7,4},{8,9},{9,10},{10,1... | collective-permute-start | bytes 98312 | tf_op jit(solution)/shard_map/ppermute | solution.py:946
  348.6 9.1 %collective-permute-start.52 = (f32[32,256]{1,0:T(8,128)S(1)}, f32[32,256]{1,0:T(8,128)S(1)}, u32[]{:S(2)}, u32[]{:S(2)}) collective-permute-start(f32[32,256]{1,0:T(8,128)S(1)} %get-tuple-element.265), channel_id=1, source_target_pairs={{0,3},{1,0},{2,1},{3,2},{4,7},{5,4},{6,5},{7,6},{8,11},{9,8},{10,9... | collective-permute-start | bytes 98312 | tf_op jit(solution)/shard_map/ppermute | solution.py:946
  (75 other events, 538.4 us)
Sparse Core Ops, SparseCore 0:
  12.6 42.3 all-gather.5
  68.3 48.6 all-gather.3
  163.0 24.2 reduce-scatter.5
  227.7 78.0 reduce-scatter.9
  309.1 24.2 reduce-scatter.7
